TPU v7x, 128 devices: a whole 4x4x4 slice. The times are simulated.
128 devices in a mesh: grp: 2 (over y_hi), row: 4 (over y_lo, core), col: 16 (over x, z).
Axes of the slice: x: 4, y: 4 (y_hi: 2, y_lo: 2; y = y_hi * 2 + y_lo), z: 4, core: 2. Of those that a mesh axis runs over, the one named last changes fastest.
Arguments:
- members: float32 [2, 2048, 2048], P('grp', 'row', 'col'), may hold values from -6 to 6
- control: float32 [2, 2048, 2048], P('grp', 'row', 'col'), may hold values from -6 to 6
- loc_spectrum: float32 [12], replicated, may hold values from 0.2 to 3
- pattern: int32 [48, 2], replicated, may hold values from 0 to 11
- shell_index: int32 [16, 16], replicated, may hold values from 0 to 11, as said below
Outputs:
- increment: float32 [2048, 2048], P('row', 'col')
Inputs may be any that keep to these rules, and one draw needn't show every extreme that they name: `shell_index`: tile (0, 0) lies in block 0, and tile (8, 8) in block 11; blocks grow with the tile's distance from wavenumber zero, give or take one.
All inputs are finite; a program needn't handle non-finite values.
Results may differ from a plain program's by a relative error of at most 0.0003.
Values sent between devices are 32-bit elements; how exact they have to be, the bound alone decides.
No kernel may reach another device: no remote copies, remote signals or barrier semaphores. Data moves between devices by JAX's collectives and lax.ppermute only.
A program may use at most 64 MiB of HBM per device.

v0:
```python
import math

import jax
import jax.numpy as jnp
import ml_dtypes
import numpy as np
from jax import lax
from jax.experimental import pallas as pl
from jax.experimental.pallas import tpu as pltpu
from jax.sharding import PartitionSpec as P

NBAND = 2
NSHELL = 12
F32 = jnp.float32
BF16 = jnp.bfloat16
C1, C2, C3 = math.cos(math.pi / 8), math.cos(math.pi / 4), math.cos(3 * math.pi / 8)
LIMIT = 48 * 1024 * 1024


def split_table(table):
    high = table.astype(ml_dtypes.bfloat16)
    low = (table - high.astype(np.float64)).astype(ml_dtypes.bfloat16)
    return high, low


def rows_tables():
    j = np.arange(128)
    full_f, full_i, half_f, half_i = [], [], [], []
    scale = 1.0 / (2048.0 * 2048.0)

    def interleave(real_part, imag_part):
        chunks = real_part.shape[0] // 16
        stacked = np.stack([real_part.reshape(chunks, 16, -1), imag_part.reshape(chunks, 16, -1)], axis=1)
        return stacked.reshape(chunks * 32, -1)

    for s in range(1, 8):
        t = np.arange(128)
        theta = 2 * np.pi * (((s + 16 * t)[:, None] * j[None, :]) % 2048) / 2048
        cos, sin = np.cos(theta), np.sin(theta)
        full_f.append(interleave(np.concatenate([cos, sin], 1), np.concatenate([-sin, cos], 1)))
        full_i.append(2 * scale * interleave(np.concatenate([cos, sin], 1), np.concatenate([-sin, cos], 1)).T)
    for s in (0, 8):
        t = np.arange(64)
        theta = 2 * np.pi * (((s + 16 * t)[:, None] * j[None, :]) % 2048) / 2048
        cos, sin = np.cos(theta), -np.sin(theta)
        weight = np.full((64, 1), 2.0)
        if s == 0:
            sin[0] = 1.0 - 2.0 * (j % 2)
            weight[0] = 1.0
        half_f.append(interleave(cos, sin))
        half_i.append(scale * interleave(weight * cos, weight * sin).T)
    return np.stack(full_f), np.stack(half_f), np.stack(full_i), np.stack(half_i)


def cols_tables():
    j = np.arange(128)
    theta = 2 * np.pi * ((j[:, None] * j[None, :]) % 128) / 128
    cos, sin = np.cos(theta), np.sin(theta)
    forward = np.block([[cos, -sin], [sin, cos]])
    inverse = np.block([[cos, sin], [-sin, cos]])
    angle = 2 * np.pi * (np.arange(16)[:, None] * j[None, :]) / 2048
    twiddle = np.stack([np.cos(angle), -np.sin(angle)], axis=1).astype(np.float32)
    return forward, inverse, twiddle


def split_value(value):
    high = value.astype(BF16)
    return high, (value - high.astype(F32)).astype(BF16)


def mxu(a, b):
    return jnp.dot(a, b, preferred_element_type=F32)


def table_times(high, low, value):
    v_high, v_low = split_value(value)
    wide = mxu(high, jnp.concatenate([v_high, v_low], axis=1))
    return wide[:, :128] + wide[:, 128:] + mxu(low, v_high)


def times_table(value, high, low):
    v_high, v_low = split_value(value)
    return mxu(v_high, high) + (mxu(v_low, high) + mxu(v_high, low))


def fft4(a, b, c, d, sign):
    s0r, s0i = a[0] + c[0], a[1] + c[1]
    s1r, s1i = a[0] - c[0], a[1] - c[1]
    s2r, s2i = b[0] + d[0], b[1] + d[1]
    s3r, s3i = b[0] - d[0], b[1] - d[1]
    rr, ri = -sign * s3i, sign * s3r
    return (
        (s0r + s2r, s0i + s2i),
        (s1r + rr, s1i + ri),
        (s0r - s2r, s0i - s2i),
        (s1r - rr, s1i - ri),
    )


def turn(z, k, sign):
    re, im = z
    k = (k * sign) % 16
    if k == 0:
        return z
    if k == 4:
        return (-im, re)
    if k == 2:
        return ((re - im) * C2, (re + im) * C2)
    if k == 14:
        return ((re + im) * C2, (im - re) * C2)
    if k == 6:
        return ((re + im) * -C2, (re - im) * C2)
    if k == 10:
        return ((im - re) * C2, (re + im) * -C2)
    cos, sin = math.cos(2 * math.pi * k / 16), math.sin(2 * math.pi * k / 16)
    return (re * cos - im * sin, re * sin + im * cos)


def fft16(z, sign):
    out = [None] * 16
    inner = [fft4(z[p], z[p + 4], z[p + 8], z[p + 12], sign) for p in range(4)]
    for k in range(4):
        outer = fft4(*[turn(inner[p][k], p * k, sign) for p in range(4)], sign)
        for q in range(4):
            out[k + 4 * q] = outer[q]
    return out


def swap_blocks(values, lane):
    low64 = lane < 64
    low32 = (lane & 32) == 0
    a0, a1, a2, a3 = values
    b0 = jnp.where(low64, a0, pltpu.roll(a2, 64, 1))
    b2 = jnp.where(low64, pltpu.roll(a0, 64, 1), a2)
    b1 = jnp.where(low64, a1, pltpu.roll(a3, 64, 1))
    b3 = jnp.where(low64, pltpu.roll(a1, 64, 1), a3)
    c0 = jnp.where(low32, b0, pltpu.roll(b1, 32, 1))
    c1 = jnp.where(low32, pltpu.roll(b0, 96, 1), b1)
    c2 = jnp.where(low32, b2, pltpu.roll(b3, 32, 1))
    c3 = jnp.where(low32, pltpu.roll(b2, 96, 1), b3)
    return c0, c1, c2, c3


def rows_forward(place, members, control, received, full_h, full_l, half_h, half_l, out, z_full, z_half):
    row = place[0]
    first = (row & 1) == 0
    flip = jnp.where((row >> 1) == 0, 1.0, -1.0).astype(F32)
    for slab in range(16):
        x = []
        for m in range(8):
            at = pl.ds((m % 4) * 128 + slab * 8, 8)
            own = jnp.where(first, members[at, :], control[at, :])
            own_here = first if m < 4 else jnp.logical_not(first)
            x.append(jnp.where(own_here, own, received[at, :]))
        e = [x[m] + x[m + 4] for m in range(4)]
        d = [x[m] - x[m + 4] for m in range(4)]
        e02, e13 = e[0] + e[2], e[1] + e[3]
        minus, plus = (d[1] - d[3]) * C2, (d[1] + d[3]) * C2
        a = [None] + [(x[m] - x[8 - m]) * flip for m in range(1, 4)]
        b = [None] + [(x[m] + x[8 - m]) * flip for m in range(1, 4)]
        x0, x4 = x[0] * flip, x[4] * flip
        even, odd = x0 + a[2] * C2, x0 - a[2] * C2
        p1, p3 = a[1] * C1 + a[3] * C3, a[1] * C3 - a[3] * C1
        i_even, i_odd = x4 + b[2] * C2, b[2] * C2 - x4
        q1, q3 = b[1] * C3 + b[3] * C1, b[1] * C1 - b[3] * C3
        rows = pl.ds(slab * 8, 8)
        shifted = pl.ds(128 + slab * 8, 8)
        z_half[0, rows, :] = e02 + e13
        z_half[1, rows, :] = e02 - e13
        values = {
            1: (even + p1, -(i_even + q1)),
            2: (d[0] + minus, -(d[2] + plus)),
            3: (odd + p3, -(i_odd + q3)),
            4: (e[0] - e[2], e[3] - e[1]),
            5: (odd - p3, i_odd - q3),
            6: (d[0] - minus, d[2] - plus),
            7: (even - p1, i_even - q1),
        }
        for s, (re, im) in values.items():
            z_full[s - 1, rows, :] = re
            z_full[s - 1, shifted, :] = im
    for s in range(7):
        out[pl.ds(256 * s, 256), :] = table_times(full_h[s], full_l[s], z_full[s])
    for s in range(2):
        out[pl.ds(1792 + 128 * s, 128), :] = table_times(half_h[s], half_l[s], z_half[s])


def gain_tables(place, pattern, loc, shell_index, straight, mirrored):
    chunk = place[1]
    general = chunk < 56
    s = jnp.where(general, (chunk >> 3) + 1, jnp.where(chunk < 60, 0, 8))
    u = jnp.where(general, chunk & 7, (chunk - 56) & 3)
    special = chunk == 56
    pairs = pattern[...]
    shell_lane = lax.broadcasted_iota(jnp.int32, (pairs.shape[0], NSHELL), 1)
    hits = pairs[:, 1:2] == shell_lane
    second = pairs[:, 0:1] * NBAND >= NSHELL
    shells = shell_index[...]
    loc_row = loc[...]
    filters = []
    in_second = shells * NBAND >= NSHELL
    filters.append(jnp.where(in_second, 0.0, 1.0).astype(F32))
    filters.append(jnp.where(in_second, 1.0, 0.0).astype(F32))
    for band in range(NBAND):
        chosen = second if band else jnp.logical_not(second)
        counts = jnp.sum(jnp.where(jnp.logical_and(hits, chosen), 1.0, 0.0).astype(F32), axis=0, keepdims=True)
        tab = counts * loc_row
        gain = jnp.zeros(shells.shape, F32)
        for shell in range(NSHELL):
            gain = jnp.where(shells == shell, tab[:, shell : shell + 1], gain)
        filters.append(gain)
    i = lax.broadcasted_iota(jnp.int32, (16, 16), 0)
    a = lax.broadcasted_iota(jnp.int32, (16, 16), 1)
    t = 16 * u + i
    tile = t >> 3
    negated = jnp.where(s == 0, ((128 - t) & 127) >> 3, 15 - tile)
    pick = (a == tile, a == negated)
    swap_row = jnp.logical_and(special, i == 0)
    partner = tuple(a == jnp.where(swap_row, 8, chosen) for chosen in (tile, negated))
    lane = lax.broadcasted_iota(jnp.int32, (16, 128), 1)
    tile_row = lax.broadcasted_iota(jnp.int32, (16, 128), 0)
    spread = tile_row == (lane >> 3)
    spread_neg = (tile_row == (((128 - lane) & 127) >> 3), tile_row == 15 - (lane >> 3))

    def as_f32(mask):
        return jnp.where(mask, 1.0, 0.0).astype(F32)

    def dot(x, y):
        return jnp.dot(x, y, preferred_element_type=F32, precision=lax.Precision.HIGHEST)

    choose = jnp.concatenate([as_f32(m) for m in pick + partner], axis=0)
    widen = jnp.concatenate([as_f32(m) for m in (spread,) + spread_neg], axis=1)
    for f in range(2 * NBAND):
        wide = dot(dot(choose, filters[f]), widen)
        for kind in range(2):
            at = slice(128 + 128 * kind, 256 + 128 * kind)
            here = 0.5 * (wide[0:16, :128] + wide[16:32, at])
            other = 0.5 * (wide[32:48, :128] + wide[48:64, at])
            straight[kind, f] = 0.5 * (here + other)
            mirrored[kind, f] = (0.5 * (here - other))[0:8]


def cols_filter(received, straight, mirrored, twiddle, fwd_h, fwd_l, inv_h, inv_l, out, z, y, v):
    tw = [(twiddle[s, 0:1, :], twiddle[s, 1:2, :]) for s in range(16)]

    def put(s, field, at, zr, zi):
        wr, wi = tw[s]
        z[s, field, at, 0:128] = zr * wr - zi * wi
        z[s, field, at, 128:256] = zr * wi + zi * wr

    for field in range(2):
        for half in range(2):
            re_at, im_at = pl.ds(8 * half, 8), pl.ds(16 + 8 * half, 8)
            values = []
            for c in range(16):
                one, two = field * 16 + c, (field + 2) * 16 + c
                values.append(
                    (received[one, re_at, :] + received[two, re_at, :], received[one, im_at, :] + received[two, im_at, :])
                )
            values = fft16(values, -1)
            for s in range(16):
                put(s, field, re_at, *values[s])
                if half == 0:
                    mr, mi = values[(16 - s) % 16]
                    put(s, field, pl.ds(16, 8), mr, -mi)
    for group in range(4):
        spectrum = times_table(z[pl.ds(4 * group, 4)].reshape(4 * 2 * 24, 256), fwd_h[...], fwd_l[...])
        spectrum = spectrum.reshape(4, 2, 24, 256)
        filtered = []
        for step in range(4):
            kind = 0 if group == 0 and step == 0 else 1
            for f in range(4):
                tile = spectrum[step, f // 2]
                gain = straight[kind, f]
                mirror = mirrored[kind, f]
                gain = jnp.concatenate([gain, gain], axis=1)
                mirror = jnp.concatenate([mirror, mirror], axis=1)
                top = gain[0:8] * tile[0:8] + mirror * tile[16:24]
                filtered.append(jnp.concatenate([top, gain[8:16] * tile[8:16]], axis=0))
        filtered = jnp.concatenate(filtered, axis=0)
        back = times_table(filtered, inv_h[...], inv_l[...])
        y[pl.ds(4 * group, 4)] = back.reshape(4, 4, 16, 256)
    lane = lax.broadcasted_iota(jnp.int32, (8, 128), 1)
    for half in range(2):
        at = pl.ds(8 * half, 8)
        for f in range(4):
            values = []
            for s in range(16):
                re, im = y[s, f, at, 0:128], y[s, f, at, 128:256]
                wr, wi = tw[s]
                values.append((re * wr + im * wi, im * wr - re * wi))
            values = fft16(values, 1)
            for c in range(16):
                v[f, c, 0] = values[c][0]
                v[f, c, 1] = values[c][1]
        for c in range(16):
            for part in range(2):
                moved = swap_blocks([v[f, c, part] for f in range(4)], lane)
                for r in range(4):
                    out[r * 16 + c, pl.ds(16 * part + 8 * half, 8), :] = moved[r]


def rows_inverse(received, full_h, full_l, half_h, half_l, out, z_full, z_half):
    for s in range(7):
        z_full[s] = table_times(full_h[s], full_l[s], received[pl.ds(256 * s, 256), :])
    for s in range(2):
        z_half[s] = table_times(half_h[s], half_l[s], received[pl.ds(1792 + 128 * s, 128), :])
    lane = lax.broadcasted_iota(jnp.int32, (8, 128), 1)
    block = lane >> 5
    for slab in range(16):
        rows, shifted = pl.ds(slab * 8, 8), pl.ds(128 + slab * 8, 8)
        y0, y8 = z_half[0, rows, :], z_half[1, rows, :]
        a = [None] + [z_full[s, rows, :] for s in range(7)]
        b = [None] + [z_full[s, shifted, :] for s in range(7)]
        plus, minus = y0 + y8, y0 - y8
        a26, turned = a[2] + a[6], (a[2] - a[6]) * C2
        c_even = [plus + a26 + a[4], minus + turned, plus - a[4], minus - turned, plus - a26 + a[4]]
        p, q, r, t = a[1] - a[7], a[3] - a[5], a[1] + a[7], a[3] + a[5]
        c_odd = [r + t, p * C1 + q * C3, (r - t) * C2, p * C3 - q * C1, None]
        b17, b35, b26 = b[1] + b[7], b[3] + b[5], (b[2] + b[6]) * C2
        d17, d35 = b[1] - b[7], b[3] - b[5]
        s_odd = [None, b17 * C3 + b35 * C1, (d17 + d35) * C2, b17 * C1 - b35 * C3, d17 - d35]
        s_even = [None, b26 + b[4], b[2] - b[6], b26 - b[4], None]
        x = [None] * 16
        for m in range(5):
            if m == 0:
                x[0], x[8] = c_even[0] + c_odd[0], c_even[0] - c_odd[0]
            elif m == 4:
                x[4], x[12] = c_even[4] - s_odd[4], c_even[4] + s_odd[4]
            else:
                c_near, c_far = c_even[m] + c_odd[m], c_even[m] - c_odd[m]
                s_near, s_far = s_odd[m] + s_even[m], s_odd[m] - s_even[m]
                x[m], x[16 - m] = c_near - s_near, c_near + s_near
                x[8 - m], x[8 + m] = c_far - s_far, c_far + s_far
        total = []
        for m in range(16):
            product = x[m] * pltpu.roll(x[m], 64, 1)
            total.append(product + pltpu.roll(product, 32, 1))
        for dest in range(4):
            packed = total[4 * dest]
            for k in range(1, 4):
                packed = jnp.where(block == k, total[4 * dest + k], packed)
            out[dest, rows, :] = packed
            out[4 + dest, rows, :] = packed


def assemble(received, out):
    lane = lax.broadcasted_iota(jnp.int32, (8, 128), 1)
    for slab in range(16):
        rows = pl.ds(slab * 8, 8)
        moved = swap_blocks([received[r, rows, :] + received[4 + r, rows, :] for r in range(4)], lane)
        for m in range(4):
            out[pl.ds(128 * m + slab * 8, 8), :] = moved[m]


def in_vmem(count):
    return [pl.BlockSpec(memory_space=pltpu.VMEM)] * count


def in_smem():
    return [pl.BlockSpec(memory_space=pltpu.SMEM)]


def params():
    return pltpu.CompilerParams(vmem_limit_bytes=LIMIT)


def shape(*dims):
    return jax.ShapeDtypeStruct(dims, F32)


def on_device(members, control, loc_spectrum, pattern, shell_index):
    row, col = lax.axis_index("row"), lax.axis_index("col")
    place = jnp.stack([row, row * 16 + col]).astype(jnp.int32)
    full_f, half_f, full_i, half_i = [split_table(t) for t in rows_tables()]
    fwd, inv, twiddle = cols_tables()
    fwd, inv = split_table(fwd), split_table(inv)
    members = members.reshape(512, 128)
    control = control.reshape(512, 128)
    send = jnp.where((row & 1) == 0, control, members)
    received = lax.ppermute(send, "row", [(0, 1), (1, 0), (2, 3), (3, 2)])
    straight, mirrored = pl.pallas_call(
        gain_tables,
        out_shape=(shape(2, 4, 16, 128), shape(2, 4, 8, 128)),
        in_specs=in_smem() + in_vmem(3),
        out_specs=tuple(in_vmem(2)),
        compiler_params=params(),
        name="gain_tables",
    )(place, pattern, loc_spectrum.reshape(1, NSHELL), shell_index)
    spectra = pl.pallas_call(
        rows_forward,
        out_shape=shape(2048, 128),
        in_specs=in_smem() + in_vmem(7),
        out_specs=in_vmem(1)[0],
        scratch_shapes=[pltpu.VMEM((7, 256, 128), F32), pltpu.VMEM((2, 128, 128), F32)],
        compiler_params=params(),
        name="rows_forward",
    )(place, members, control, received, *full_f, *half_f)
    spectra = lax.all_to_all(spectra.reshape(64, 32, 128), ("row", "col"), split_axis=0, concat_axis=0, tiled=True)
    filtered = pl.pallas_call(
        cols_filter,
        out_shape=shape(64, 32, 128),
        in_specs=in_vmem(8),
        out_specs=in_vmem(1)[0],
        scratch_shapes=[
            pltpu.VMEM((16, 2, 24, 256), F32),
            pltpu.VMEM((16, 4, 16, 256), F32),
            pltpu.VMEM((4, 16, 2, 8, 128), F32),
        ],
        compiler_params=params(),
        name="cols_filter",
    )(spectra, straight, mirrored, twiddle, *fwd, *inv)
    filtered = lax.all_to_all(filtered, ("row", "col"), split_axis=0, concat_axis=0, tiled=True)
    products = pl.pallas_call(
        rows_inverse,
        out_shape=shape(8, 128, 128),
        in_specs=in_vmem(5),
        out_specs=in_vmem(1)[0],
        scratch_shapes=[pltpu.VMEM((7, 256, 128), F32), pltpu.VMEM((2, 128, 128), F32)],
        compiler_params=params(),
        name="rows_inverse",
    )(filtered.reshape(2048, 128), *full_i, *half_i)
    products = lax.all_to_all(products, ("grp", "row"), split_axis=0, concat_axis=0, tiled=True)
    return pl.pallas_call(
        assemble,
        out_shape=shape(512, 128),
        in_specs=in_vmem(1),
        out_specs=in_vmem(1)[0],
        compiler_params=params(),
        name="assemble",
    )(products)


def solution(mesh):
    placed = (P("grp", "row", "col"), P("grp", "row", "col"), P(), P(), P())
    return jax.shard_map(
        on_device, mesh=mesh, in_specs=placed, out_specs=P("row", "col"), check_vma=False
    )
```

profile of v0, /device:TPU:0, one launch (start us, length us, event | category | flops | bytes accessed | tf_op | source)
XLA Modules:
  0.0 76.0 jit_solution(5486847158420102750)
XLA Ops:
  0.0 1.1 %broadcast_select_fusion = f32[512,128]{1,0:T(8,128)S(1)} fusion(pred[]{:T(512)S(6)} %eq.3, f32[1,512,128]{2,1,0:T(8,128)} %param.19, f32[1,512,128]{2,1,0:T(8,128)} %param.18), kind=kLoop, calls=%fused_computation | loop fusion | flops 65536 | bytes 786433 | tf_op jit(solution)/shard_map/jit(_where)/select_n | solution.py:380
  1.1 0.1 collective-permute-start
  1.2 0.1 pad_add_fusion.place
  1.3 1.4 %collective-permute-done.received = f32[512,128]{1,0:T(8,128)S(1)} collective-permute-done((f32[512,128]{1,0:T(8,128)S(1)}, f32[512,128]{1,0:T(8,128)S(1)}, u32[]{:S(2)}, u32[]{:S(2)}) %collective-permute-start) | collective-permute-done | bytes 262176 | tf_op jit(solution)/shard_map/ppermute | solution.py:381
  2.8 0.0 copy-start.4
  2.8 1.2 %copy-done.4 = bf16[7,256,256]{2,1,0:T(8,128)(2,1)S(1)} copy-done((bf16[7,256,256]{2,1,0:T(8,128)(2,1)S(1)}, bf16[7,256,256]{2,1,0:T(8,128)(2,1)}, u32[]{:S(2)}) %copy-start.4) | copy-done | bytes 917528
  4.0 1.2 %copy-done.5 = bf16[7,256,256]{2,1,0:T(8,128)(2,1)S(1)} copy-done((bf16[7,256,256]{2,1,0:T(8,128)(2,1)S(1)}, bf16[7,256,256]{2,1,0:T(8,128)(2,1)}, u32[]{:S(2)}) %copy-start.5) | copy-done | bytes 917528
  5.1 2.3 %rows_forward.1 = f32[2048,128]{1,0:T(8,128)} custom-call(s32[2]{0:T(128)S(1)} %pad_add_fusion.place, f32[512,128]{1,0:T(8,128)S(1)} %bitcast.10, f32[512,128]{1,0:T(8,128)S(1)} %bitcast.11, f32[512,128]{1,0:T(8,128)S(1)} %collective-permute-done.received, bf16[7,256,256]{2,1,0:T(8,128)(2,1)S(1)} %copy-done.4, bf16[7,256,256]{2,1,0:T(8,128)(2,1)S(1)} %copy-done.5, ...), custom_call_target="tpu_custom_call" | custom-call | tf_op jit(solution)/shard_map/rows_forward/pallas_call | solution.py:390
  7.5 0.0 copy-start.9
  7.5 10.0 %all-to-all-start = ((f32[64,32,128]{2,1,0:T(8,128)}), f32[64,32,128]{2,1,0:T(8,128)S(1)}, u32[]{:S(2)}, u32[]{:S(2)}) async-start(f32[64,32,128]{2,1,0:T(8,128)} %bitcast.4), calls=%async_computation | async-start | bytes 2097152 | tf_op jit(solution)/shard_map/all_to_all | solution.py:399
  17.6 0.1 copy.19.pattern
  17.6 0.6 copy-done.15
  18.2 0.1 copy-done.16
  18.3 1.7 %gain_tables.1 = (f32[2,4,16,128]{3,2,1,0:T(8,128)S(1)}, f32[2,4,8,128]{3,2,1,0:T(8,128)S(1)}) custom-call(s32[2]{0:T(128)S(1)} %pad_add_fusion.place, s32[48,2]{1,0:T(8,128)S(1)} %copy.19.pattern, f32[1,12]{1,0:T(1,128)S(1)} %bitcast.12, s32[16,16]{1,0:T(8,128)S(1)} %copy-done.15), custom_call_target="tpu_custom_call" | custom-call | tf_op jit(solution)/shard_map/gain_tables/pallas_call | solution.py:382
  20.0 15.3 %all-to-all-done.received = f32[64,32,128]{2,1,0:T(8,128)S(1)} async-done(((f32[64,32,128]{2,1,0:T(8,128)}), f32[64,32,128]{2,1,0:T(8,128)S(1)}, u32[]{:S(2)}, u32[]{:S(2)}) %all-to-all-start) | async-done | bytes 1048608 | tf_op jit(solution)/shard_map/all_to_all | solution.py:399
  35.3 1.9 %cols_filter.1 = f32[64,32,128]{2,1,0:T(8,128)S(1)} custom-call(f32[64,32,128]{2,1,0:T(8,128)S(1)} %all-to-all-done.received, f32[2,4,16,128]{3,2,1,0:T(8,128)S(1)} %get-tuple-element.7.straight, f32[2,4,8,128]{3,2,1,0:T(8,128)S(1)} %get-tuple-element.8.mirrored, f32[16,2,128]{2,1,0:T(2,128)S(1)} %copy-done.14, bf16[256,256]{1,0:T(8,128)(2,1)S(1)} %copy-done.6, ...), custom_call_target="tpu_custom_call" | custom-call | tf_op jit(solution)/shard_map/cols_filter/pallas_call | solution.py:400
  37.2 0.0 copy-start.2
  37.2 0.0 copy-start.3
  37.2 0.0 copy-start.10
  37.2 0.0 copy-start.11
  37.2 22.0 %all_to_all.15 = f32[64,32,128]{2,1,0:T(8,128)S(1)} all-to-all(f32[64,32,128]{2,1,0:T(8,128)S(1)} %cols_filter.1), channel_id=1, replica_groups=mesh['grp'=2,'row'=4,'col'=16] {'row','col'}, dimensions={0} | all-to-all | bytes 2097152 | tf_op jit(solution)/shard_map/all_to_all | solution.py:413
  59.3 1.3 %rows_inverse.1 = f32[8,128,128]{2,1,0:T(8,128)S(1)} custom-call(f32[2048,128]{1,0:T(8,128)S(1)} %bitcast.9, bf16[7,256,256]{2,1,0:T(8,128)(2,1)S(1)} %copy-done.2, bf16[7,256,256]{2,1,0:T(8,128)(2,1)S(1)} %copy-done.3, bf16[2,128,128]{2,1,0:T(8,128)(2,1)S(1)} %copy-done.10, bf16[2,128,128]{2,1,0:T(8,128)(2,1)S(1)} %copy-done.11), custom_call_target="tpu_custom_call" | custom-call | tf_op jit(solution)/shard_map/rows_inverse/pallas_call | solution.py:414
  60.6 14.4 %all_to_all.16.received = f32[8,128,128]{2,1,0:T(8,128)S(1)} all-to-all(f32[8,128,128]{2,1,0:T(8,128)S(1)} %rows_inverse.1), channel_id=1, replica_groups=mesh['grp'=2,'row'=4,'col'=16] {'grp','row'}, dimensions={0} | all-to-all | bytes 1048576 | tf_op jit(solution)/shard_map/all_to_all | solution.py:423
  75.0 1.0 %assemble.1 = f32[512,128]{1,0:T(8,128)} custom-call(f32[8,128,128]{2,1,0:T(8,128)S(1)} %all_to_all.16.received), custom_call_target="tpu_custom_call" | custom-call | tf_op jit(solution)/shard_map/assemble/pallas_call | solution.py:424
  (26 shorter events, 0.1 us)
Async XLA Ops:
  0.0 2.8 %copy-start = (f32[1,512,128]{2,1,0:T(8,128)S(1)}, f32[1,512,128]{2,1,0:T(8,128)}, u32[]{:S(2)}) copy-start(f32[1,512,128]{2,1,0:T(8,128)} %param.18) | copy-start | bytes 786436
  0.0 2.8 %copy-start.1 = (f32[1,512,128]{2,1,0:T(8,128)S(1)}, f32[1,512,128]{2,1,0:T(8,128)}, u32[]{:S(2)}) copy-start(f32[1,512,128]{2,1,0:T(8,128)} %param.19) | copy-start | bytes 786436
  0.0 2.8 %copy-start.12 = (bf16[2,128,128]{2,1,0:T(8,128)(2,1)S(1)}, bf16[2,128,128]{2,1,0:T(8,128)(2,1)}, u32[]{:S(2)}) copy-start(bf16[2,128,128]{2,1,0:T(8,128)(2,1)} %constant.43.clone.half_h) | copy-start | bytes 196612
  0.0 2.8 %copy-start.13 = (bf16[2,128,128]{2,1,0:T(8,128)(2,1)S(1)}, bf16[2,128,128]{2,1,0:T(8,128)(2,1)}, u32[]{:S(2)}) copy-start(bf16[2,128,128]{2,1,0:T(8,128)(2,1)} %constant.44.clone.half_l) | copy-start | bytes 196612
  1.1 1.6 %collective-permute-start = (f32[512,128]{1,0:T(8,128)S(1)}, f32[512,128]{1,0:T(8,128)S(1)}, u32[]{:S(2)}, u32[]{:S(2)}) collective-permute-start(f32[512,128]{1,0:T(8,128)S(1)} %broadcast_select_fusion), channel_id=1, source_target_pairs={{0,16},{16,0},{32,48},{48,32},{1,17},{17,1},{33,49},{49,33},{2,18}... | collective-permute-start | bytes 786440 | tf_op jit(solution)/shard_map/ppermute | solution.py:381
  2.8 1.2 %copy-start.4 = (bf16[7,256,256]{2,1,0:T(8,128)(2,1)S(1)}, bf16[7,256,256]{2,1,0:T(8,128)(2,1)}, u32[]{:S(2)}) copy-start(bf16[7,256,256]{2,1,0:T(8,128)(2,1)} %constant.41.clone.full_h) | copy-start | bytes 2752516
  4.0 1.2 %copy-start.5 = (bf16[7,256,256]{2,1,0:T(8,128)(2,1)S(1)}, bf16[7,256,256]{2,1,0:T(8,128)(2,1)}, u32[]{:S(2)}) copy-start(bf16[7,256,256]{2,1,0:T(8,128)(2,1)} %constant.42.clone.full_l) | copy-start | bytes 2752516
  7.5 10.1 %copy-start.17 = (s32[48,2]{0,1:T(2,128)S(1)}, s32[48,2]{0,1:T(2,128)}, u32[]{:S(2)}) copy-start(s32[48,2]{0,1:T(2,128)} %param.21) | copy-start | bytes 1156
  7.5 27.8 %copy-start.6 = (bf16[256,256]{1,0:T(8,128)(2,1)S(1)}, bf16[256,256]{1,0:T(8,128)(2,1)}, u32[]{:S(2)}) copy-start(bf16[256,256]{1,0:T(8,128)(2,1)} %constant.46.clone.fwd_h) | copy-start | bytes 393220
  7.5 27.8 %copy-start.7 = (bf16[256,256]{1,0:T(8,128)(2,1)S(1)}, bf16[256,256]{1,0:T(8,128)(2,1)}, u32[]{:S(2)}) copy-start(bf16[256,256]{1,0:T(8,128)(2,1)} %constant.47.clone.fwd_l) | copy-start | bytes 393220
  7.5 27.8 %copy-start.8 = (bf16[256,256]{1,0:T(8,128)(2,1)S(1)}, bf16[256,256]{1,0:T(8,128)(2,1)}, u32[]{:S(2)}) copy-start(bf16[256,256]{1,0:T(8,128)(2,1)} %constant.48.clone.inv_h) | copy-start | bytes 393220
  7.5 27.8 %copy-start.9 = (bf16[256,256]{1,0:T(8,128)(2,1)S(1)}, bf16[256,256]{1,0:T(8,128)(2,1)}, u32[]{:S(2)}) copy-start(bf16[256,256]{1,0:T(8,128)(2,1)} %constant.49.clone.inv_l) | copy-start | bytes 393220
  7.5 27.8 %all-to-all-start = ((f32[64,32,128]{2,1,0:T(8,128)}), f32[64,32,128]{2,1,0:T(8,128)S(1)}, u32[]{:S(2)}, u32[]{:S(2)}) async-start(f32[64,32,128]{2,1,0:T(8,128)} %bitcast.4), calls=%async_computation | async-start | bytes 2097152 | tf_op jit(solution)/shard_map/all_to_all | solution.py:399
  17.5 0.7 copy-start.15
  17.6 0.7 copy-start.16
  18.3 17.0 %copy-start.14 = (f32[16,2,128]{2,1,0:T(2,128)S(1)}, f32[16,2,128]{2,1,0:T(2,128)}, u32[]{:S(2)}) copy-start(f32[16,2,128]{2,1,0:T(2,128)} %constant.45.clone.twiddle) | copy-start | bytes 49156
  37.2 22.1 %copy-start.2 = (bf16[7,256,256]{2,1,0:T(8,128)(2,1)S(1)}, bf16[7,256,256]{2,1,0:T(8,128)(2,1)}, u32[]{:S(2)}) copy-start(bf16[7,256,256]{2,1,0:T(8,128)(2,1)} %constant.50.clone.full_h) | copy-start | bytes 2752516
  37.2 22.1 %copy-start.3 = (bf16[7,256,256]{2,1,0:T(8,128)(2,1)S(1)}, bf16[7,256,256]{2,1,0:T(8,128)(2,1)}, u32[]{:S(2)}) copy-start(bf16[7,256,256]{2,1,0:T(8,128)(2,1)} %constant.51.clone.full_l) | copy-start | bytes 2752516
  37.2 22.1 %copy-start.10 = (bf16[2,128,128]{2,1,0:T(8,128)(2,1)S(1)}, bf16[2,128,128]{2,1,0:T(8,128)(2,1)}, u32[]{:S(2)}) copy-start(bf16[2,128,128]{2,1,0:T(8,128)(2,1)} %constant.52.clone.half_h) | copy-start | bytes 196612
  37.2 22.1 %copy-start.11 = (bf16[2,128,128]{2,1,0:T(8,128)(2,1)S(1)}, bf16[2,128,128]{2,1,0:T(8,128)(2,1)}, u32[]{:S(2)}) copy-start(bf16[2,128,128]{2,1,0:T(8,128)(2,1)} %constant.53.clone.half_l) | copy-start | bytes 196612
where the time goes:
time: 76.8 us; the launch traced here: 76 us
  blocking collectives  36.4 us (47%)
  waiting for transfers between devices  16.8 us (22%)
  starting transfers between devices  10.1 us (13%)
  Pallas kernels  8.17 us (11%)
  local copies, waits for them, and re-layouts  3.17 us (4%)
  other arithmetic  1.2 us (2%)
    all_to_all x1, blocking collectives, on_device(): lax.all_to_all(filtered, ('row', 'col'), split_axis=0, concat_axis=0, til...  22 us
    all_to_all x1, waiting for transfers between devices, on_device(): lax.all_to_all(spectra.reshape(64, 32, 128), ('row', 'col'), split_axis=0...  15.3 us
    all_to_all x1, blocking collectives, on_device(): lax.all_to_all(products, ('grp', 'row'), split_axis=0, concat_axis=0, til...  14.4 us
    all_to_all x1, starting transfers between devices, on_device(): lax.all_to_all(spectra.reshape(64, 32, 128), ('row', 'col'), split_axis=0...  10 us
    unnamed x37, local copies, waits for them, and re-layouts  3.17 us
    pallas_call x1, Pallas kernels, on_device(): pl.pallas_call(rows_forward, out_shape=shape(2048, 128), in_specs=in_smem...  2.33 us
    pallas_call x1, Pallas kernels, on_device(): pl.pallas_call(cols_filter, out_shape=shape(64, 32, 128), in_specs=in_vme...  1.86 us
    pallas_call x1, Pallas kernels, on_device(): pl.pallas_call(gain_tables, out_shape=(shape(2, 4, 16, 128), shape(2, 4,...  1.66 us
  transfers between devices with their start and end apart: 2, of which 2 were waited for; matrix products, arithmetic and copies ran while one was open for 0% of the time, Pallas kernels for 2%

commit v1 on v0

v1 whole, which is shorter than its diff:
```python
import math

import jax
import jax.numpy as jnp
import ml_dtypes
import numpy as np
from jax import lax
from jax.experimental import pallas as pl
from jax.experimental.pallas import tpu as pltpu
from jax.sharding import PartitionSpec as P

NBAND = 2
NSHELL = 12
F32 = jnp.float32
BF16 = jnp.bfloat16
C1, C2, C3 = math.cos(math.pi / 8), math.cos(math.pi / 4), math.cos(3 * math.pi / 8)
LIMIT = 48 * 1024 * 1024
SCALE = 1.0 / (2048.0 * 2048.0)


def split_table(table):
    high = table.astype(ml_dtypes.bfloat16)
    low = (table - high.astype(np.float64)).astype(ml_dtypes.bfloat16)
    return high, low


def rows_tables():
    j = np.arange(128)
    t = np.arange(64)
    forward, inverse = [], []

    def interleave(real_part, imag_part):
        stacked = np.stack([real_part.reshape(4, 16, 128), imag_part.reshape(4, 16, 128)], axis=1)
        return stacked.reshape(128, 128)

    for s in (0, 8):
        theta = 2 * np.pi * (((s + 16 * t)[:, None] * j[None, :]) % 2048) / 2048
        cos, sin = np.cos(theta), -np.sin(theta)
        weight = np.full((64, 1), 2.0)
        if s == 0:
            sin[0] = 1.0 - 2.0 * (j % 2)
            weight[0] = 1.0
        forward.append(interleave(cos, sin))
        inverse.append(SCALE * interleave(weight * cos, weight * sin).T)
    return np.stack(forward), np.stack(inverse)


def cols_tables():
    j = np.arange(128)
    theta = 2 * np.pi * ((j[:, None] * j[None, :]) % 128) / 128
    cos, sin = np.cos(theta), np.sin(theta)
    forward = np.block([[cos, -sin], [sin, cos]])
    inverse = np.block([[cos, sin], [-sin, cos]])
    angle = 2 * np.pi * (np.arange(16)[:, None] * j[None, :]) / 2048
    twiddle = np.stack([np.cos(angle), -np.sin(angle)], axis=1).astype(np.float32)
    column = np.concatenate([np.cos(angle[:8]), np.sin(angle[:8])], axis=0).T
    return forward, inverse, twiddle, column


def split_value(value):
    high = value.astype(BF16)
    return high, (value - high.astype(F32)).astype(BF16)


def mxu(a, b):
    return jnp.dot(a, b, preferred_element_type=F32)


def table_times(both, value):
    v_high, v_low = split_value(value)
    rows = both.shape[0] // 2
    first = mxu(both, v_high)
    return first[:rows] + (first[rows:] + mxu(both[:rows], v_low))


def times_table(value, both):
    v_high, v_low = split_value(value)
    high, low = both[:256], both[256:]
    return mxu(v_high, high) + (mxu(v_low, high) + mxu(v_high, low))


def fft4(a, b, c, d, sign):
    s0r, s0i = a[0] + c[0], a[1] + c[1]
    s1r, s1i = a[0] - c[0], a[1] - c[1]
    s2r, s2i = b[0] + d[0], b[1] + d[1]
    s3r, s3i = b[0] - d[0], b[1] - d[1]
    rr, ri = -sign * s3i, sign * s3r
    return (
        (s0r + s2r, s0i + s2i),
        (s1r + rr, s1i + ri),
        (s0r - s2r, s0i - s2i),
        (s1r - rr, s1i - ri),
    )


def turn(z, k, sign):
    re, im = z
    k = (k * sign) % 16
    if k == 0:
        return z
    if k == 4:
        return (-im, re)
    if k == 2:
        return ((re - im) * C2, (re + im) * C2)
    if k == 14:
        return ((re + im) * C2, (im - re) * C2)
    if k == 6:
        return ((re + im) * -C2, (re - im) * C2)
    if k == 10:
        return ((im - re) * C2, (re + im) * -C2)
    cos, sin = math.cos(2 * math.pi * k / 16), math.sin(2 * math.pi * k / 16)
    return (re * cos - im * sin, re * sin + im * cos)


def fft16(z, sign):
    out = [None] * 16
    inner = [fft4(z[p], z[p + 4], z[p + 8], z[p + 12], sign) for p in range(4)]
    for k in range(4):
        outer = fft4(*[turn(inner[p][k], p * k, sign) for p in range(4)], sign)
        for q in range(4):
            out[k + 4 * q] = outer[q]
    return out


def swap_blocks(values, lane):
    values = list(values)
    low = lane < 64
    for i in range(4):
        one, two = values[i], values[i + 4]
        moved = pltpu.roll(jnp.where(low, two, one), 64, 1)
        values[i], values[i + 4] = jnp.where(low, one, moved), jnp.where(low, moved, two)
    for d in (2, 1):
        low = (lane & (16 * d)) == 0
        for i in range(8):
            if i & d:
                continue
            one, two = values[i], values[i + d]
            values[i] = jnp.where(low, one, pltpu.roll(two, 16 * d, 1))
            values[i + d] = jnp.where(low, pltpu.roll(one, 128 - 16 * d, 1), two)
    return values


def rows_forward(own, got_members, got_control, tables, columns, out, z_full, z_half):
    row = lax.axis_index("row")
    first = (row & 1) == 0
    flip = jnp.where((row >> 1) == 0, 1.0, -1.0).astype(F32)
    for slab in range(16):
        x = []
        for m in range(8):
            at = pl.ds((m % 4) * 128 + slab * 8, 8)
            if m < 4:
                x.append(jnp.where(first, own[at, :], got_control[at, :]))
            else:
                x.append(jnp.where(first, got_members[at, :], own[at, :]))
        e = [x[m] + x[m + 4] for m in range(4)]
        d = [x[m] - x[m + 4] for m in range(4)]
        e02, e13 = e[0] + e[2], e[1] + e[3]
        minus, plus = (d[1] - d[3]) * C2, (d[1] + d[3]) * C2
        a = [None] + [(x[m] - x[8 - m]) * flip for m in range(1, 4)]
        b = [None] + [(x[m] + x[8 - m]) * flip for m in range(1, 4)]
        x0, x4 = x[0] * flip, x[4] * flip
        even, odd = x0 + a[2] * C2, x0 - a[2] * C2
        p1, p3 = a[1] * C1 + a[3] * C3, a[1] * C3 - a[3] * C1
        i_even, i_odd = x4 + b[2] * C2, b[2] * C2 - x4
        q1, q3 = b[1] * C3 + b[3] * C1, b[1] * C1 - b[3] * C3
        rows = pl.ds(slab * 8, 8)
        shifted = pl.ds(128 + slab * 8, 8)
        z_half[0, rows, :] = e02 + e13
        z_half[1, rows, :] = e02 - e13
        values = {
            1: (even + p1, -(i_even + q1)),
            2: (d[0] + minus, -(d[2] + plus)),
            3: (odd + p3, -(i_odd + q3)),
            4: (e[0] - e[2], e[3] - e[1]),
            5: (odd - p3, i_odd - q3),
            6: (d[0] - minus, d[2] - plus),
            7: (even - p1, i_even - q1),
        }
        turns = columns[rows, 0:16]
        for s, (re, im) in values.items():
            cos, sin = turns[:, s : s + 1], turns[:, 8 + s : 9 + s]
            lanes = pl.ds(128 * (s - 1), 128)
            z_full[rows, lanes] = re * cos + im * sin
            z_full[shifted, lanes] = im * cos - re * sin
    for pair in range(4):
        width = 256 if pair < 3 else 128
        result = table_times(tables[0:512, :], z_full[:, 256 * pair : 256 * pair + width])
        for k in range(width // 128):
            at = 256 * (2 * pair + k)
            lanes = slice(128 * k, 128 * k + 128)
            for u in range(8):
                out[pl.ds(at + 32 * u, 16), :] = result[16 * u : 16 * u + 16, lanes]
                out[pl.ds(at + 32 * u + 16, 16), :] = result[128 + 16 * u : 144 + 16 * u, lanes]
    for s in range(2):
        out[pl.ds(1792 + 128 * s, 128), :] = table_times(tables[1024:1280, 128 * s : 128 * s + 128], z_half[s])


def front(members, control, tables, columns, pattern, loc, shell_index, own, tables_v, columns_v, straight, mirrored,
          pairs_v, loc_v, shells_v, sems):
    row, col = lax.axis_index("row"), lax.axis_index("col")
    first = (row & 1) == 0
    field = pltpu.make_async_copy(members, own, sems.at[0])
    small = [
        pltpu.make_async_copy(pattern, pairs_v, sems.at[3]),
        pltpu.make_async_copy(loc, loc_v, sems.at[4]),
        pltpu.make_async_copy(shell_index, shells_v, sems.at[5]),
    ]
    large = [
        pltpu.make_async_copy(tables, tables_v, sems.at[1]),
        pltpu.make_async_copy(columns, columns_v, sems.at[2]),
    ]
    for copy in small:
        copy.start()

    @pl.when(first)
    def _():
        field.start()

    @pl.when(jnp.logical_not(first))
    def _():
        pltpu.make_async_copy(control, own, sems.at[0]).start()

    for copy in large:
        copy.start()
    for copy in small:
        copy.wait()
    chunk = row * 16 + col
    general = chunk < 56
    s = jnp.where(general, (chunk >> 3) + 1, jnp.where(chunk < 60, 0, 8))
    u = jnp.where(general, chunk & 7, (chunk - 56) & 3)
    special = chunk == 56
    from_shell, to_shell = pairs_v[0:1, :], pairs_v[1:2, :]
    hits = to_shell == lax.broadcasted_iota(jnp.int32, (NSHELL, to_shell.shape[1]), 0)
    second = from_shell * NBAND >= NSHELL
    shells = shells_v[...]
    in_second = shells * NBAND >= NSHELL
    filters = [jnp.where(in_second, 0.0, 1.0).astype(F32), jnp.where(in_second, 1.0, 0.0).astype(F32)]
    for band in range(NBAND):
        chosen = second if band else jnp.logical_not(second)
        counts = jnp.sum(jnp.where(jnp.logical_and(hits, chosen), 1.0, 0.0).astype(F32), axis=1, keepdims=True)
        gain = jnp.zeros(shells.shape, F32)
        for shell in range(NSHELL):
            gain = jnp.where(shells == shell, counts[shell : shell + 1, :] * loc_v[:, shell : shell + 1], gain)
        filters.append(gain)
    i = lax.broadcasted_iota(jnp.int32, (16, 16), 0)
    a = lax.broadcasted_iota(jnp.int32, (16, 16), 1)
    t = 16 * u + i
    tile = t >> 3
    negated = jnp.where(s == 0, ((128 - t) & 127) >> 3, 15 - tile)
    pick = (a == tile, a == negated)
    swap_row = jnp.logical_and(special, i == 0)
    partner = tuple(a == jnp.where(swap_row, 8, chosen) for chosen in (tile, negated))
    lane = lax.broadcasted_iota(jnp.int32, (16, 128), 1)
    tile_row = lax.broadcasted_iota(jnp.int32, (16, 128), 0)
    spread = tile_row == (lane >> 3)
    spread_neg = (tile_row == (((128 - lane) & 127) >> 3), tile_row == 15 - (lane >> 3))

    def as_f32(mask):
        return jnp.where(mask, 1.0, 0.0).astype(F32)

    def dot(x, y):
        return jnp.dot(x, y, preferred_element_type=F32, precision=lax.Precision.HIGHEST)

    choose = jnp.concatenate([as_f32(m) for m in pick + partner], axis=0)
    widen = jnp.concatenate([as_f32(m) for m in (spread,) + spread_neg], axis=1)
    for f in range(2 * NBAND):
        wide = dot(dot(choose, filters[f]), widen)
        for kind in range(2):
            at = slice(128 + 128 * kind, 256 + 128 * kind)
            here = 0.5 * (wide[0:16, :128] + wide[16:32, at])
            other = 0.5 * (wide[32:48, :128] + wide[48:64, at])
            straight[kind, f] = 0.5 * (here + other)
            mirrored[kind, f] = (0.5 * (here - other))[0:8]
    field.wait()
    for copy in large:
        copy.wait()


def cols_filter(received, straight, mirrored, tables, columns, out, z, y, v):
    tw = [(columns[128 + s : 129 + s, :], columns[144 + s : 145 + s, :]) for s in range(16)]

    def put(s, field, at, zr, zi):
        wr, wi = tw[s]
        z[s, field, at, 0:128] = zr * wr - zi * wi
        z[s, field, at, 128:256] = zr * wi + zi * wr

    for field in range(2):
        for half in range(2):
            re_at, im_at = pl.ds(8 * half, 8), pl.ds(16 + 8 * half, 8)
            values = []
            for c in range(16):
                one, two = field * 16 + c, (field + 2) * 16 + c
                values.append(
                    (received[one, re_at, :] + received[two, re_at, :], received[one, im_at, :] + received[two, im_at, :])
                )
            values = fft16(values, -1)
            for s in range(16):
                put(s, field, re_at, *values[s])
                if half == 0:
                    mr, mi = values[(16 - s) % 16]
                    put(s, field, pl.ds(16, 8), mr, -mi)
    for group in range(4):
        spectrum = times_table(z[pl.ds(4 * group, 4)].reshape(4 * 2 * 24, 256), tables[512:1024, :])
        spectrum = spectrum.reshape(4, 2, 24, 256)
        filtered = []
        for step in range(4):
            kind = 0 if group == 0 and step == 0 else 1
            for f in range(4):
                tile = spectrum[step, f // 2]
                gain = straight[kind, f]
                mirror = mirrored[kind, f]
                gain = jnp.concatenate([gain, gain], axis=1)
                mirror = jnp.concatenate([mirror, mirror], axis=1)
                top = gain[0:8] * tile[0:8] + mirror * tile[16:24]
                filtered.append(jnp.concatenate([top, gain[8:16] * tile[8:16]], axis=0))
        filtered = jnp.concatenate(filtered, axis=0)
        back = times_table(filtered, tables[0:512, :])
        y[pl.ds(4 * group, 4)] = back.reshape(4, 4, 16, 256)
    lane = lax.broadcasted_iota(jnp.int32, (8, 128), 1)
    for half in range(2):
        at = pl.ds(8 * half, 8)
        for f in range(4):
            values = []
            for s in range(16):
                re, im = y[s, f, at, 0:128], y[s, f, at, 128:256]
                wr, wi = tw[s]
                values.append((re * wr + im * wi, im * wr - re * wi))
            values = fft16(values, 1)
            for c in range(16):
                v[f, c, 0] = values[c][0]
                v[f, c, 1] = values[c][1]
        for c in range(16):
            moved = swap_blocks([v[f, c, part] for f in range(4) for part in range(2)], lane)
            for q in range(8):
                out[q * 16 + c, at, :] = moved[q]


def rows_inverse(received, tables, columns, out, z_full, z_half):
    row = lax.axis_index("row")
    lane16 = lax.broadcasted_iota(jnp.int32, (16, 128), 1)
    even = (lane16 & 16) == 0

    def chunk(d):
        one, two = received[d], received[64 + d]
        re = jnp.where(even, one, pltpu.roll(two, 16, 1))
        im = jnp.where(even, pltpu.roll(one, 112, 1), two)
        return re, im

    for pair in range(4):
        spectra = []
        for s in range(2 * pair, min(2 * pair + 2, 7)):
            parts = [chunk(8 * s + u) for u in range(8)]
            spectra.append(jnp.concatenate([p[0] for p in parts] + [p[1] for p in parts], axis=0))
        result = table_times(tables[512:1024, :], jnp.concatenate(spectra, axis=1) if len(spectra) > 1 else spectra[0])
        for k in range(len(spectra)):
            z_full[2 * pair + k] = result[:, 128 * k : 128 * k + 128]
    for s in range(2):
        parts = [chunk(56 + 4 * s + u) for u in range(4)]
        z_half[s] = table_times(tables[1280:1536, 128 * s : 128 * s + 128], jnp.concatenate([p[k] for p in parts for k in range(2)], axis=0))
    lane = lax.broadcasted_iota(jnp.int32, (8, 128), 1)
    low64, low32, low16 = lane < 64, (lane & 32) == 0, (lane & 16) == 0

    def fold(one, two, low, shift):
        other = jnp.where(low, two, one)
        return jnp.where(low, one, two) + jnp.where(low, pltpu.roll(other, 128 - shift, 1), pltpu.roll(other, shift, 1))

    for slab in range(8):
        x = [fields_of(slab + 8 * h, z_full, z_half, columns) for h in range(2)]
        for dest in range(4):
            u = []
            for m in range(4 * dest, 4 * dest + 4):
                one, two = x[0][m], x[1][m]
                u.append(jnp.where(low64, one, two) * pltpu.roll(jnp.where(low64, two, one), 64, 1))
            packed = fold(fold(u[0], u[2], low32, 32), fold(u[1], u[3], low32, 32), low16, 16)
            slot = dest ^ row
            out[((slot & 1) << 1) | (slot >> 1), pl.ds(slab * 8, 8), :] = packed


def fields_of(slab, z_full, z_half, columns):
    rows, shifted = pl.ds(slab * 8, 8), pl.ds(128 + slab * 8, 8)
    y0, y8 = z_half[0, rows, :], z_half[1, rows, :]
    turns = columns[rows, 16:32]
    a, b = [None], [None]
    for s in range(1, 8):
        cos, sin = turns[:, s : s + 1], turns[:, 8 + s : 9 + s]
        re, im = z_full[s - 1, rows, :], z_full[s - 1, shifted, :]
        a.append(re * cos - im * sin)
        b.append(re * sin + im * cos)
    plus, minus = y0 + y8, y0 - y8
    a26, turned = a[2] + a[6], (a[2] - a[6]) * C2
    c_even = [plus + a26 + a[4], minus + turned, plus - a[4], minus - turned, plus - a26 + a[4]]
    p, q, r, t = a[1] - a[7], a[3] - a[5], a[1] + a[7], a[3] + a[5]
    c_odd = [r + t, p * C1 + q * C3, (r - t) * C2, p * C3 - q * C1, None]
    b17, b35, b26 = b[1] + b[7], b[3] + b[5], (b[2] + b[6]) * C2
    d17, d35 = b[1] - b[7], b[3] - b[5]
    s_odd = [None, b17 * C3 + b35 * C1, (d17 + d35) * C2, b17 * C1 - b35 * C3, d17 - d35]
    s_even = [None, b26 + b[4], b[2] - b[6], b26 - b[4], None]
    x = [None] * 16
    x[0], x[8] = c_even[0] + c_odd[0], c_even[0] - c_odd[0]
    x[4], x[12] = c_even[4] - s_odd[4], c_even[4] + s_odd[4]
    for m in range(1, 4):
        c_near, c_far = c_even[m] + c_odd[m], c_even[m] - c_odd[m]
        s_near, s_far = s_odd[m] + s_even[m], s_odd[m] - s_even[m]
        x[m], x[16 - m] = c_near - s_near, c_near + s_near
        x[8 - m], x[8 + m] = c_far - s_far, c_far + s_far
    return x


def assemble(own, by_row, by_grp, by_both, out, pieces):
    mine = lax.axis_index("grp") * 4 + lax.axis_index("row")
    for k, ref in enumerate((own, by_row, by_grp, by_both)):
        pieces[pl.ds(2 * k, 2)] = ref[...]
    lane = lax.broadcasted_iota(jnp.int32, (8, 128), 1)
    for slab in range(8):
        rows = pl.ds(slab * 8, 8)
        moved = swap_blocks([pieces[q ^ mine, rows, :] for q in range(8)], lane)
        for e in range(8):
            out[pl.ds(128 * (e & 3) + 64 * (e >> 2) + slab * 8, 8), :] = moved[e]


def in_vmem(count):
    return [pl.BlockSpec(memory_space=pltpu.VMEM)] * count


def in_hbm(*arrays):
    return [pltpu.with_memory_space_constraint(jnp.asarray(x), pltpu.HBM) for x in arrays]


def params():
    return pltpu.CompilerParams(vmem_limit_bytes=LIMIT)


def shape(*dims):
    return jax.ShapeDtypeStruct(dims, F32)


def constant_tables():
    half_f, half_i = [np.concatenate(split_table(t), axis=1) for t in rows_tables()]
    fwd, inv, twiddle, column = cols_tables()
    halves = [np.concatenate([h[0], h[1]], axis=1) for h in (half_f, half_i)]
    tables = np.concatenate([*split_table(inv), *split_table(fwd), *halves], axis=0)
    columns = np.zeros((160, 128), np.float32)
    columns[:128, 0:16] = column
    columns[:128, 16:32] = 2 * SCALE * column
    columns[128:144] = twiddle[:, 0]
    columns[144:160] = twiddle[:, 1]
    return tables, columns


def on_device(members, control, loc_spectrum, pattern, shell_index):
    tables, columns = constant_tables()
    members = members.reshape(512, 128)
    control = control.reshape(512, 128)
    swap_cores = [(0, 1), (1, 0), (2, 3), (3, 2)]
    got_members = lax.ppermute(members, "row", swap_cores)
    got_control = lax.ppermute(control, "row", swap_cores)
    own, tables, columns, straight, mirrored = pl.pallas_call(
        front,
        out_shape=(
            shape(512, 128),
            jax.ShapeDtypeStruct(tables.shape, BF16),
            shape(*columns.shape),
            shape(2, 4, 16, 128),
            shape(2, 4, 8, 128),
        ),
        in_specs=[pl.BlockSpec(memory_space=pltpu.HBM)] * 7,
        out_specs=tuple(in_vmem(5)),
        scratch_shapes=[
            pltpu.VMEM((2, pattern.shape[0]), jnp.int32),
            pltpu.VMEM((1, NSHELL), F32),
            pltpu.VMEM(shell_index.shape, jnp.int32),
            pltpu.SemaphoreType.DMA((6,)),
        ],
        compiler_params=params(),
        name="front",
    )(*in_hbm(members, control, tables, columns, pattern.T, loc_spectrum.reshape(1, NSHELL), shell_index))
    spectra = pl.pallas_call(
        rows_forward,
        out_shape=shape(2048, 128),
        in_specs=in_vmem(5),
        out_specs=in_vmem(1)[0],
        scratch_shapes=[pltpu.VMEM((256, 896), F32), pltpu.VMEM((2, 128, 128), F32)],
        compiler_params=params(),
        name="rows_forward",
    )(own, got_members, got_control, tables, columns)
    spectra = lax.all_to_all(spectra.reshape(64, 32, 128), ("row", "col"), split_axis=0, concat_axis=0, tiled=True)
    filtered = pl.pallas_call(
        cols_filter,
        out_shape=shape(128, 16, 128),
        in_specs=in_vmem(5),
        out_specs=in_vmem(1)[0],
        scratch_shapes=[
            pltpu.VMEM((16, 2, 24, 256), F32),
            pltpu.VMEM((16, 4, 16, 256), F32),
            pltpu.VMEM((4, 16, 2, 8, 128), F32),
        ],
        compiler_params=params(),
        name="cols_filter",
    )(spectra, straight, mirrored, tables, columns)
    filtered = lax.all_to_all(filtered, ("grp", "row", "col"), split_axis=0, concat_axis=0, tiled=True)
    products = pl.pallas_call(
        rows_inverse,
        out_shape=shape(4, 64, 128),
        in_specs=in_vmem(3),
        out_specs=in_vmem(1)[0],
        scratch_shapes=[pltpu.VMEM((7, 256, 128), F32), pltpu.VMEM((2, 128, 128), F32)],
        compiler_params=params(),
        name="rows_inverse",
    )(filtered, tables, columns)
    got = lax.ppermute(products[2:4], "row", swap_cores)
    near = jnp.stack([products[0], got[0]])
    far = jnp.stack([products[1], got[1]])

    def exchange(value, step):
        return lax.ppermute(value, ("grp", "row"), [(i, i ^ step) for i in range(8)])

    by_grp, by_both, by_row = exchange(near, 4), exchange(far, 6), exchange(far, 2)
    return pl.pallas_call(
        assemble,
        out_shape=shape(512, 128),
        in_specs=in_vmem(4),
        out_specs=in_vmem(1)[0],
        scratch_shapes=[pltpu.VMEM((8, 64, 128), F32)],
        compiler_params=params(),
        name="assemble",
    )(near, by_row, by_grp, by_both)


def solution(mesh):
    placed = (P("grp", "row", "col"), P("grp", "row", "col"), P(), P(), P())
    return jax.shard_map(
        on_device, mesh=mesh, in_specs=placed, out_specs=P("row", "col"), check_vma=False
    )
```

time: 76.8 us -> 70.1 us (0.913)
  blocking collectives: 36.4 us -> 52.7 us
  waiting for transfers between devices: 16.8 us -> 5.31 us
  starting transfers between devices: 10.1 us -> 4.16 us
  local copies, waits for them, and re-layouts: 3.17 us -> 0.02 us
  other arithmetic: 1.2 us -> 0.01 us
  Pallas kernels: 8.17 us -> 7.36 us
    all_to_all x2, blocking collectives: 36.4 us -> 52.7 us  [the longest x1 27.4 us: on_device(): lax.all_to_all(spectra.reshape(64, 32, 128), ('row', 'col'), split_axis=0...]
    all_to_all x1 -> x0, waiting for transfers between devices: 15.3 us -> none  [on_device(): lax.all_to_all(spectra.reshape(64, 32, 128), ('row', 'col'), split_axis=0...]
    all_to_all x1 -> x0, starting transfers between devices: 10 us -> none  [on_device(): lax.all_to_all(spectra.reshape(64, 32, 128), ('row', 'col'), split_axis=0...]
    ppermute x1 -> x6, starting transfers between devices: 0.09 us -> 4.16 us  [the longest x3 3.57 us: exchange(): lax.ppermute(value, ('grp', 'row'), [(i, i ^ step) for i in range(8)])]
    ppermute x1 -> x6, waiting for transfers between devices: 1.44 us -> 5.31 us  [the longest x3 4.08 us: exchange(): lax.ppermute(value, ('grp', 'row'), [(i, i ^ step) for i in range(8)])]
    unnamed x37 -> x0, local copies, waits for them, and re-layouts: 3.17 us -> none
    select_n x1 -> x0, other arithmetic: 1.12 us -> none  [on_device(): send = jnp.where(row & 1 == 0, control, members)]
    pallas_call x5, Pallas kernels: 8.17 us -> 7.36 us  [the longest x1 2 us: on_device(): pl.pallas_call(cols_filter, out_shape=shape(128, 16, 128), in_specs=in_vm...]
  transfers between devices with their start and end apart: 2 -> 6, of which waited for: 2 -> 4; matrix products, arithmetic and copies ran while one was open for 0% -> 0% of each run, Pallas kernels for 2% -> 3%
where the time goes in v1:
time: 70.1 us; the launch traced here: 69.6 us
  blocking collectives  52.7 us (75%)
  Pallas kernels  7.36 us (10%)
  waiting for transfers between devices  5.31 us (8%)
  starting transfers between devices  4.16 us (6%)
    all_to_all x1, blocking collectives, on_device(): lax.all_to_all(spectra.reshape(64, 32, 128), ('row', 'col'), split_axis=0...  27.4 us
    all_to_all x1, blocking collectives, on_device(): lax.all_to_all(filtered, ('grp', 'row', 'col'), split_axis=0, concat_axis...  25.2 us
    ppermute x3, waiting for transfers between devices, exchange(): lax.ppermute(value, ('grp', 'row'), [(i, i ^ step) for i in range(8)])  4.08 us
    ppermute x3, starting transfers between devices, exchange(): lax.ppermute(value, ('grp', 'row'), [(i, i ^ step) for i in range(8)])  3.57 us
    pallas_call x1, Pallas kernels, on_device(): pl.pallas_call(cols_filter, out_shape=shape(128, 16, 128), in_specs=in_vm...  2 us
    pallas_call x1, Pallas kernels, on_device(): pl.pallas_call(front, out_shape=(shape(512, 128), jax.ShapeDtypeStruct(ta...  1.9 us
    pallas_call x1, Pallas kernels, on_device(): pl.pallas_call(rows_inverse, out_shape=shape(4, 64, 128), in_specs=in_vme...  1.52 us
  transfers between devices with their start and end apart: 6, of which 4 were waited for; matrix products, arithmetic and copies ran while one was open for 0% of the time, Pallas kernels for 3%

profile of v1, /device:TPU:0, one launch (start us, length us, event | category | flops | bytes accessed | tf_op | source)
XLA Modules:
  0.0 69.6 jit_solution(11489714313836774124)
XLA Ops:
  0.0 0.0 collective-permute-start
  0.0 0.5 collective-permute-start.1
  0.5 1.9 %front.1 = (f32[512,128]{1,0:T(8,128)S(1)}, bf16[1536,256]{1,0:T(8,128)(2,1)S(1)}, f32[160,128]{1,0:T(8,128)S(1)}, f32[2,4,16,128]{3,2,1,0:T(8,128)S(1)}, f32[2,4,8,128]{3,2,1,0:T(8,128)S(1)}) custom-call(f32[512,128]{1,0:T(8,128)} %bitcast.7, f32[512,128]{1,0:T(8,128)} %bitcast.9, bf16[1536,256]{1,0:T(8,128)(2,1)} %constant.4.clone.tables, ...), custom_call_target="tpu_custom_call" | custom-call | tf_op jit(solution)/shard_map/front/pallas_call | solution.py:457
  2.4 0.0 collective-permute-done.got_members
  2.4 0.0 collective-permute-done.1.got_control
  2.4 1.0 %rows_forward.1 = f32[2048,128]{1,0:T(8,128)S(1)} custom-call(f32[512,128]{1,0:T(8,128)S(1)} %get-tuple-element.10.own, f32[512,128]{1,0:T(8,128)S(1)} %collective-permute-done.got_members, f32[512,128]{1,0:T(8,128)S(1)} %collective-permute-done.1.got_control, bf16[1536,256]{1,0:T(8,128)(2,1)S(1)} %get-tuple-element.11.tables, ...), custom_call_target="tpu_custom_call" | custom-call | tf_op jit(solution)/shard_map/rows_forward/pallas_call | solution.py:477
  3.4 27.4 %all_to_all.10.received = f32[64,32,128]{2,1,0:T(8,128)S(1)} all-to-all(f32[64,32,128]{2,1,0:T(8,128)S(1)} %bitcast.5), channel_id=1, replica_groups=mesh['grp'=2,'row'=4,'col'=16] {'row','col'}, dimensions={0} | all-to-all | bytes 2097152 | tf_op jit(solution)/shard_map/all_to_all | solution.py:486
  30.8 2.0 %cols_filter.1 = f32[128,16,128]{2,1,0:T(8,128)S(1)} custom-call(f32[64,32,128]{2,1,0:T(8,128)S(1)} %all_to_all.10.received, f32[2,4,16,128]{3,2,1,0:T(8,128)S(1)} %get-tuple-element.13.straight, f32[2,4,8,128]{3,2,1,0:T(8,128)S(1)} %get-tuple-element.14.mirrored, bf16[1536,256]{1,0:T(8,128)(2,1)S(1)} %get-tuple-element.11.tables, ...), custom_call_target="tpu_custom_call" | custom-call | tf_op jit(solution)/shard_map/cols_filter/pallas_call | solution.py:487
  32.8 25.2 %all_to_all.11.received = f32[128,16,128]{2,1,0:T(8,128)S(1)} all-to-all(f32[128,16,128]{2,1,0:T(8,128)S(1)} %cols_filter.1), channel_id=1, replica_groups=mesh['grp'=2,'row'=4,'col'=16] {'grp','row','col'}, dimensions={0} | all-to-all | bytes 2097152 | tf_op jit(solution)/shard_map/all_to_all | solution.py:500
  58.1 1.5 %rows_inverse.1 = f32[4,64,128]{2,1,0:T(8,128)S(1)} custom-call(f32[128,16,128]{2,1,0:T(8,128)S(1)} %all_to_all.11.received, bf16[1536,256]{1,0:T(8,128)(2,1)S(1)} %get-tuple-element.11.tables, f32[160,128]{1,0:T(8,128)S(1)} %get-tuple-element.12.columns), custom_call_target="tpu_custom_call" | custom-call | tf_op jit(solution)/shard_map/rows_inverse/pallas_call | solution.py:501
  59.6 0.1 collective-permute-start.2
  59.7 1.2 %collective-permute-done.2 = f32[2,64,128]{2,1,0:T(8,128)S(1)} collective-permute-done((f32[2,64,128]{2,1,0:T(8,128)S(1)}, f32[2,64,128]{2,1,0:T(8,128)S(1)}, u32[]{:S(2)}, u32[]{:S(2)}) %collective-permute-start.2) | collective-permute-done | bytes 65568 | tf_op jit(solution)/shard_map/ppermute | solution.py:510
  61.0 0.9 %collective-permute-start.4 = (f32[2,64,128]{2,1,0:T(8,128)S(1)}, f32[2,64,128]{2,1,0:T(8,128)S(1)}, u32[]{:S(2)}, u32[]{:S(2)}) collective-permute-start(f32[2,64,128]{2,1,0:T(8,128)S(1)} %pad_maximum_fusion.own), channel_id=1, source_target_pairs={{0,64},{16,80},{32,96},{48,112},{64,0},{80,16},{96,32},{112,48},{1... | collective-permute-start | bytes 196616 | tf_op jit(solution)/shard_map/ppermute | solution.py:515
  61.9 2.5 %collective-permute-start.5 = (f32[2,64,128]{2,1,0:T(8,128)S(1)}, f32[2,64,128]{2,1,0:T(8,128)S(1)}, u32[]{:S(2)}, u32[]{:S(2)}) collective-permute-start(f32[2,64,128]{2,1,0:T(8,128)S(1)} %pad_maximum_fusion.1), channel_id=1, source_target_pairs={{0,96},{16,112},{32,64},{48,80},{64,32},{80,48},{96,0},{112,16},{1... | collective-permute-start | bytes 196616 | tf_op jit(solution)/shard_map/ppermute | solution.py:515
  64.4 0.2 collective-permute-start.3
  64.5 2.4 %collective-permute-done.4.by_grp = f32[2,64,128]{2,1,0:T(8,128)S(1)} collective-permute-done((f32[2,64,128]{2,1,0:T(8,128)S(1)}, f32[2,64,128]{2,1,0:T(8,128)S(1)}, u32[]{:S(2)}, u32[]{:S(2)}) %collective-permute-start.4) | collective-permute-done | bytes 65568 | tf_op jit(solution)/shard_map/ppermute | solution.py:515
  66.9 1.2 %collective-permute-done.5.by_both = f32[2,64,128]{2,1,0:T(8,128)S(1)} collective-permute-done((f32[2,64,128]{2,1,0:T(8,128)S(1)}, f32[2,64,128]{2,1,0:T(8,128)S(1)}, u32[]{:S(2)}, u32[]{:S(2)}) %collective-permute-start.5) | collective-permute-done | bytes 65568 | tf_op jit(solution)/shard_map/ppermute | solution.py:515
  68.1 0.5 collective-permute-done.3.by_row
  68.6 1.0 %assemble.1 = f32[512,128]{1,0:T(8,128)} custom-call(f32[2,64,128]{2,1,0:T(8,128)S(1)} %pad_maximum_fusion.own, f32[2,64,128]{2,1,0:T(8,128)S(1)} %collective-permute-done.3.by_row, f32[2,64,128]{2,1,0:T(8,128)S(1)} %collective-permute-done.4.by_grp, f32[2,64,128]{2,1,0:T(8,128)S(1)} %collective-permute-done.5.by_both), custom_call_target="tpu_custom_call" | custom-call | tf_op jit(solution)/shard_map/assemble/pallas_call | solution.py:518
  (5 shorter events, 0.0 us)
Async XLA Ops:
  0.0 2.4 %collective-permute-start = (f32[512,128]{1,0:T(8,128)}, f32[512,128]{1,0:T(8,128)S(1)}, u32[]{:S(2)}, u32[]{:S(2)}) collective-permute-start(f32[512,128]{1,0:T(8,128)} %bitcast.6), channel_id=1, source_target_pairs={{0,16},{16,0},{32,48},{48,32},{1,17},{17,1},{33,49},{49,33},{2,18}... | collective-permute-start | bytes 786440 | tf_op jit(solution)/shard_map/ppermute | solution.py:455
  0.0 2.4 %collective-permute-start.1 = (f32[512,128]{1,0:T(8,128)}, f32[512,128]{1,0:T(8,128)S(1)}, u32[]{:S(2)}, u32[]{:S(2)}) collective-permute-start(f32[512,128]{1,0:T(8,128)} %bitcast.8), channel_id=1, source_target_pairs={{0,16},{16,0},{32,48},{48,32},{1,17},{17,1},{33,49},{49,33},{2,18}... | collective-permute-start | bytes 786440 | tf_op jit(solution)/shard_map/ppermute | solution.py:456
  59.6 1.3 %collective-permute-start.2 = (f32[2,64,128]{2,1,0:T(8,128)S(1)}, f32[2,64,128]{2,1,0:T(8,128)S(1)}, u32[]{:S(2)}, u32[]{:S(2)}) collective-permute-start(f32[2,64,128]{2,1,0:T(8,128)S(1)} %slice.21), channel_id=1, source_target_pairs={{0,16},{16,0},{32,48},{48,32},{1,17},{17,1},{33,49},{49,33},{2,18}... | collective-permute-start | bytes 196616 | tf_op jit(solution)/shard_map/ppermute | solution.py:510
  61.0 6.0 %collective-permute-start.4 = (f32[2,64,128]{2,1,0:T(8,128)S(1)}, f32[2,64,128]{2,1,0:T(8,128)S(1)}, u32[]{:S(2)}, u32[]{:S(2)}) collective-permute-start(f32[2,64,128]{2,1,0:T(8,128)S(1)} %pad_maximum_fusion.own), channel_id=1, source_target_pairs={{0,64},{16,80},{32,96},{48,112},{64,0},{80,16},{96,32},{112,48},{1... | collective-permute-start | bytes 196616 | tf_op jit(solution)/shard_map/ppermute | solution.py:515
  61.9 6.2 %collective-permute-start.5 = (f32[2,64,128]{2,1,0:T(8,128)S(1)}, f32[2,64,128]{2,1,0:T(8,128)S(1)}, u32[]{:S(2)}, u32[]{:S(2)}) collective-permute-start(f32[2,64,128]{2,1,0:T(8,128)S(1)} %pad_maximum_fusion.1), channel_id=1, source_target_pairs={{0,96},{16,112},{32,64},{48,80},{64,32},{80,48},{96,0},{112,16},{1... | collective-permute-start | bytes 196616 | tf_op jit(solution)/shard_map/ppermute | solution.py:515
  64.4 4.3 %collective-permute-start.3 = (f32[2,64,128]{2,1,0:T(8,128)S(1)}, f32[2,64,128]{2,1,0:T(8,128)S(1)}, u32[]{:S(2)}, u32[]{:S(2)}) collective-permute-start(f32[2,64,128]{2,1,0:T(8,128)S(1)} %pad_maximum_fusion.1), channel_id=1, source_target_pairs={{0,32},{16,48},{32,0},{48,16},{64,96},{80,112},{96,64},{112,80},{1... | collective-permute-start | bytes 196616 | tf_op jit(solution)/shard_map/ppermute | solution.py:515

commit v2 on v1

--- a/solution.py
+++ b/solution.py
@@ -7,6 +7,7 @@
 from jax import lax
 from jax.experimental import pallas as pl
 from jax.experimental.pallas import tpu as pltpu
+from jax.sharding import Mesh
 from jax.sharding import PartitionSpec as P
 
 NBAND = 2
@@ -55,6 +56,30 @@
     twiddle = np.stack([np.cos(angle), -np.sin(angle)], axis=1).astype(np.float32)
     column = np.concatenate([np.cos(angle[:8]), np.sin(angle[:8])], axis=0).T
     return forward, inverse, twiddle, column
+
+
+AXES = ("grp", "ylo", "core", "x1", "x0", "z1", "z0")
+FIRST = ("x1", "x0", "core", "z1", "ylo", "z0")
+SECOND = ("core", "z1", "z0", "x1", "x0", "grp", "ylo")
+
+
+def place_of(order, at):
+    place = 0
+    for axis in order:
+        place = place * 2 + at[axis]
+    return place
+
+
+def block_at(block):
+    return {"x1": block >> 3, "x0": (block >> 2) & 1, "z1": (block >> 1) & 1, "z0": block & 1}
+
+
+def of_group(grp, chunk):
+    at = {"grp": grp}
+    for axis in reversed(FIRST):
+        at[axis] = chunk & 1
+        chunk >>= 1
+    return place_of(SECOND, at)
 
 
 def split_value(value):
@@ -141,9 +166,8 @@
 
 
 def rows_forward(own, got_members, got_control, tables, columns, out, z_full, z_half):
-    row = lax.axis_index("row")
-    first = (row & 1) == 0
-    flip = jnp.where((row >> 1) == 0, 1.0, -1.0).astype(F32)
+    first = lax.axis_index("core") == 0
+    flip = jnp.where(lax.axis_index("ylo") == 0, 1.0, -1.0).astype(F32)
     for slab in range(16):
         x = []
         for m in range(8):
@@ -197,8 +221,8 @@
 
 def front(members, control, tables, columns, pattern, loc, shell_index, own, tables_v, columns_v, straight, mirrored,
           pairs_v, loc_v, shells_v, sems):
-    row, col = lax.axis_index("row"), lax.axis_index("col")
-    first = (row & 1) == 0
+    core = lax.axis_index("core")
+    first = core == 0
     field = pltpu.make_async_copy(members, own, sems.at[0])
     small = [
         pltpu.make_async_copy(pattern, pairs_v, sems.at[3]),
@@ -224,7 +248,7 @@
         copy.start()
     for copy in small:
         copy.wait()
-    chunk = row * 16 + col
+    chunk = place_of(FIRST, {axis: lax.axis_index(axis) for axis in FIRST})
     general = chunk < 56
     s = jnp.where(general, (chunk >> 3) + 1, jnp.where(chunk < 60, 0, 8))
     u = jnp.where(general, chunk & 7, (chunk - 56) & 3)
@@ -289,7 +313,7 @@
             re_at, im_at = pl.ds(8 * half, 8), pl.ds(16 + 8 * half, 8)
             values = []
             for c in range(16):
-                one, two = field * 16 + c, (field + 2) * 16 + c
+                one, two = [place_of(FIRST, {"ylo": ylo, "core": field, **block_at(c)}) for ylo in range(2)]
                 values.append(
                     (received[one, re_at, :] + received[two, re_at, :], received[one, im_at, :] + received[two, im_at, :])
                 )
@@ -332,16 +356,17 @@
         for c in range(16):
             moved = swap_blocks([v[f, c, part] for f in range(4) for part in range(2)], lane)
             for q in range(8):
-                out[q * 16 + c, at, :] = moved[q]
+                target = {"grp": q >> 2, "ylo": (q >> 1) & 1, "core": q & 1, **block_at(c)}
+                out[place_of(SECOND, target), at, :] = moved[q]
 
 
 def rows_inverse(received, tables, columns, out, z_full, z_half):
-    row = lax.axis_index("row")
+    row = lax.axis_index("ylo") * 2 + lax.axis_index("core")
     lane16 = lax.broadcasted_iota(jnp.int32, (16, 128), 1)
     even = (lane16 & 16) == 0
 
     def chunk(d):
-        one, two = received[d], received[64 + d]
+        one, two = received[of_group(0, d)], received[of_group(1, d)]
         re = jnp.where(even, one, pltpu.roll(two, 16, 1))
         im = jnp.where(even, pltpu.roll(one, 112, 1), two)
         return re, im
@@ -407,7 +432,7 @@
 
 
 def assemble(own, by_row, by_grp, by_both, out, pieces):
-    mine = lax.axis_index("grp") * 4 + lax.axis_index("row")
+    mine = (lax.axis_index("grp") * 2 + lax.axis_index("ylo")) * 2 + lax.axis_index("core")
     for k, ref in enumerate((own, by_row, by_grp, by_both)):
         pieces[pl.ds(2 * k, 2)] = ref[...]
     lane = lax.broadcasted_iota(jnp.int32, (8, 128), 1)
@@ -447,13 +472,65 @@
     return tables, columns
 
 
+def call_rows_forward(own, got_members, got_control, tables, columns):
+    return pl.pallas_call(
+        rows_forward,
+        out_shape=shape(2048, 128),
+        in_specs=in_vmem(5),
+        out_specs=in_vmem(1)[0],
+        scratch_shapes=[pltpu.VMEM((256, 896), F32), pltpu.VMEM((2, 128, 128), F32)],
+        compiler_params=params(),
+        name="rows_forward",
+    )(own, got_members, got_control, tables, columns)
+
+
+def call_cols_filter(spectra, straight, mirrored, tables, columns):
+    return pl.pallas_call(
+        cols_filter,
+        out_shape=shape(128, 16, 128),
+        in_specs=in_vmem(5),
+        out_specs=in_vmem(1)[0],
+        scratch_shapes=[
+            pltpu.VMEM((16, 2, 24, 256), F32),
+            pltpu.VMEM((16, 4, 16, 256), F32),
+            pltpu.VMEM((4, 16, 2, 8, 128), F32),
+        ],
+        compiler_params=params(),
+        name="cols_filter",
+    )(spectra, straight, mirrored, tables, columns)
+
+
+def call_rows_inverse(filtered, tables, columns):
+    return pl.pallas_call(
+        rows_inverse,
+        out_shape=shape(4, 64, 128),
+        in_specs=in_vmem(3),
+        out_specs=in_vmem(1)[0],
+        scratch_shapes=[pltpu.VMEM((7, 256, 128), F32), pltpu.VMEM((2, 128, 128), F32)],
+        compiler_params=params(),
+        name="rows_inverse",
+    )(filtered, tables, columns)
+
+
+def call_assemble(near, by_row, by_grp, by_both):
+    return pl.pallas_call(
+        assemble,
+        out_shape=shape(512, 128),
+        in_specs=in_vmem(4),
+        out_specs=in_vmem(1)[0],
+        scratch_shapes=[pltpu.VMEM((8, 64, 128), F32)],
+        compiler_params=params(),
+        name="assemble",
+    )(near, by_row, by_grp, by_both)
+
+
 def on_device(members, control, loc_spectrum, pattern, shell_index):
     tables, columns = constant_tables()
     members = members.reshape(512, 128)
     control = control.reshape(512, 128)
-    swap_cores = [(0, 1), (1, 0), (2, 3), (3, 2)]
-    got_members = lax.ppermute(members, "row", swap_cores)
-    got_control = lax.ppermute(control, "row", swap_cores)
+    swap_cores = [(0, 1), (1, 0)]
+    got_members = lax.ppermute(members, "core", swap_cores)
+    got_control = lax.ppermute(control, "core", swap_cores)
     own, tables, columns, straight, mirrored = pl.pallas_call(
         front,
         out_shape=(
@@ -474,60 +551,24 @@
         compiler_params=params(),
         name="front",
     )(*in_hbm(members, control, tables, columns, pattern.T, loc_spectrum.reshape(1, NSHELL), shell_index))
-    spectra = pl.pallas_call(
-        rows_forward,
-        out_shape=shape(2048, 128),
-        in_specs=in_vmem(5),
-        out_specs=in_vmem(1)[0],
-        scratch_shapes=[pltpu.VMEM((256, 896), F32), pltpu.VMEM((2, 128, 128), F32)],
-        compiler_params=params(),
-        name="rows_forward",
-    )(own, got_members, got_control, tables, columns)
-    spectra = lax.all_to_all(spectra.reshape(64, 32, 128), ("row", "col"), split_axis=0, concat_axis=0, tiled=True)
-    filtered = pl.pallas_call(
-        cols_filter,
-        out_shape=shape(128, 16, 128),
-        in_specs=in_vmem(5),
-        out_specs=in_vmem(1)[0],
-        scratch_shapes=[
-            pltpu.VMEM((16, 2, 24, 256), F32),
-            pltpu.VMEM((16, 4, 16, 256), F32),
-            pltpu.VMEM((4, 16, 2, 8, 128), F32),
-        ],
-        compiler_params=params(),
-        name="cols_filter",
-    )(spectra, straight, mirrored, tables, columns)
-    filtered = lax.all_to_all(filtered, ("grp", "row", "col"), split_axis=0, concat_axis=0, tiled=True)
-    products = pl.pallas_call(
-        rows_inverse,
-        out_shape=shape(4, 64, 128),
-        in_specs=in_vmem(3),
-        out_specs=in_vmem(1)[0],
-        scratch_shapes=[pltpu.VMEM((7, 256, 128), F32), pltpu.VMEM((2, 128, 128), F32)],
-        compiler_params=params(),
-        name="rows_inverse",
-    )(filtered, tables, columns)
-    got = lax.ppermute(products[2:4], "row", swap_cores)
+    spectra = call_rows_forward(own, got_members, got_control, tables, columns)
+    spectra = lax.all_to_all(spectra.reshape(64, 32, 128), FIRST, split_axis=0, concat_axis=0, tiled=True)
+    filtered = call_cols_filter(spectra, straight, mirrored, tables, columns)
+    filtered = lax.all_to_all(filtered, SECOND, split_axis=0, concat_axis=0, tiled=True)
+    products = call_rows_inverse(filtered, tables, columns)
+    got = lax.ppermute(products[2:4], "core", swap_cores)
     near = jnp.stack([products[0], got[0]])
     far = jnp.stack([products[1], got[1]])
 
     def exchange(value, step):
-        return lax.ppermute(value, ("grp", "row"), [(i, i ^ step) for i in range(8)])
-
-    by_grp, by_both, by_row = exchange(near, 4), exchange(far, 6), exchange(far, 2)
-    return pl.pallas_call(
-        assemble,
-        out_shape=shape(512, 128),
-        in_specs=in_vmem(4),
-        out_specs=in_vmem(1)[0],
-        scratch_shapes=[pltpu.VMEM((8, 64, 128), F32)],
-        compiler_params=params(),
-        name="assemble",
-    )(near, by_row, by_grp, by_both)
+        return lax.ppermute(value, ("grp", "ylo"), [(i, i ^ step) for i in range(4)])
+
+    by_grp, by_both, by_row = exchange(near, 2), exchange(far, 3), exchange(far, 1)
+    return call_assemble(near, by_row, by_grp, by_both)
 
 
 def solution(mesh):
-    placed = (P("grp", "row", "col"), P("grp", "row", "col"), P(), P(), P())
-    return jax.shard_map(
-        on_device, mesh=mesh, in_specs=placed, out_specs=P("row", "col"), check_vma=False
-    )
+    fine = Mesh(mesh.devices.reshape((2,) * len(AXES)), AXES)
+    rows, cols = AXES[1:3], AXES[3:]
+    placed = (P("grp", rows, cols), P("grp", rows, cols), P(), P(), P())
+    return jax.shard_map(on_device, mesh=fine, in_specs=placed, out_specs=P(rows, cols), check_vma=False)

time: 70.1 us -> 68.5 us (0.977)
  blocking collectives: 52.7 us -> 51.2 us
    all_to_all x2, blocking collectives: 52.7 us -> 51.2 us  [the longest x1 26.5 us: on_device(): lax.all_to_all(spectra.reshape(64, 32, 128), FIRST, split_axis=0, concat_...]
where the time goes in v2:
time: 68.5 us; the launch traced here: 68.3 us
  blocking collectives  51.2 us (75%)
  Pallas kernels  7.37 us (11%)
  waiting for transfers between devices  5.49 us (8%)
  starting transfers between devices  4.22 us (6%)
    all_to_all x1, blocking collectives, on_device(): lax.all_to_all(spectra.reshape(64, 32, 128), FIRST, split_axis=0, concat_...  26.5 us
    all_to_all x1, blocking collectives, on_device(): lax.all_to_all(filtered, SECOND, split_axis=0, concat_axis=0, tiled=True)  24.6 us
    ppermute x3, waiting for transfers between devices, exchange(): lax.ppermute(value, ('grp', 'ylo'), [(i, i ^ step) for i in range(4)])  4.26 us
    ppermute x3, starting transfers between devices, exchange(): lax.ppermute(value, ('grp', 'ylo'), [(i, i ^ step) for i in range(4)])  3.62 us
    pallas_call x1, Pallas kernels, call_cols_filter(): pl.pallas_call(cols_filter, out_shape=shape(128, 16, 128), in_specs=in_vm...  2 us
    pallas_call x1, Pallas kernels, on_device(): pl.pallas_call(front, out_shape=(shape(512, 128), jax.ShapeDtypeStruct(ta...  1.91 us
    pallas_call x1, Pallas kernels, call_rows_inverse(): pl.pallas_call(rows_inverse, out_shape=shape(4, 64, 128), in_specs=in_vme...  1.51 us
  transfers between devices with their start and end apart: 6, of which 4 were waited for; matrix products, arithmetic and copies ran while one was open for 0% of the time, Pallas kernels for 3%

profile of v2, /device:TPU:0, one launch (start us, length us, event | category | flops | bytes accessed | tf_op | source)
XLA Modules:
  0.0 68.3 jit_solution(17746788649002204125)
XLA Ops:
  0.0 0.0 collective-permute-start
  0.0 0.5 collective-permute-start.1
  0.5 1.9 %front.1 = (f32[512,128]{1,0:T(8,128)S(1)}, bf16[1536,256]{1,0:T(8,128)(2,1)S(1)}, f32[160,128]{1,0:T(8,128)S(1)}, f32[2,4,16,128]{3,2,1,0:T(8,128)S(1)}, f32[2,4,8,128]{3,2,1,0:T(8,128)S(1)}) custom-call(f32[512,128]{1,0:T(8,128)} %bitcast.7, f32[512,128]{1,0:T(8,128)} %bitcast.9, bf16[1536,256]{1,0:T(8,128)(2,1)} %constant.4.clone.tables, ...), custom_call_target="tpu_custom_call" | custom-call | tf_op jit(solution)/shard_map/front/pallas_call | solution.py:534
  2.4 0.0 collective-permute-done.got_members
  2.4 0.0 collective-permute-done.1.got_control
  2.4 1.0 %rows_forward.1 = f32[2048,128]{1,0:T(8,128)S(1)} custom-call(f32[512,128]{1,0:T(8,128)S(1)} %get-tuple-element.10.own, f32[512,128]{1,0:T(8,128)S(1)} %collective-permute-done.got_members, f32[512,128]{1,0:T(8,128)S(1)} %collective-permute-done.1.got_control, bf16[1536,256]{1,0:T(8,128)(2,1)S(1)} %get-tuple-element.11.tables, ...), custom_call_target="tpu_custom_call" | custom-call | tf_op jit(solution)/shard_map/rows_forward/pallas_call | solution.py:476
  3.4 26.5 %all_to_all.10.received = f32[64,32,128]{2,1,0:T(8,128)S(1)} all-to-all(f32[64,32,128]{2,1,0:T(8,128)S(1)} %bitcast.5), channel_id=1, replica_groups=mesh['grp'=2,'ylo'=2,'core'=2,'x1'=2,'x0'=2,'z1'=2,'z0'=2] {'x1','x0','c..., dimensions={0} | all-to-all | bytes 2097152 | tf_op jit(solution)/shard_map/all_to_all | solution.py:555
  29.9 2.0 %cols_filter.1 = f32[128,16,128]{2,1,0:T(8,128)S(1)} custom-call(f32[64,32,128]{2,1,0:T(8,128)S(1)} %all_to_all.10.received, f32[2,4,16,128]{3,2,1,0:T(8,128)S(1)} %get-tuple-element.13.straight, f32[2,4,8,128]{3,2,1,0:T(8,128)S(1)} %get-tuple-element.14.mirrored, bf16[1536,256]{1,0:T(8,128)(2,1)S(1)} %get-tuple-element.11.tables, ...), custom_call_target="tpu_custom_call" | custom-call | tf_op jit(solution)/shard_map/cols_filter/pallas_call | solution.py:488
  32.0 24.6 %all_to_all.11.received = f32[128,16,128]{2,1,0:T(8,128)S(1)} all-to-all(f32[128,16,128]{2,1,0:T(8,128)S(1)} %cols_filter.1), channel_id=1, replica_groups=mesh['grp'=2,'ylo'=2,'core'=2,'x1'=2,'x0'=2,'z1'=2,'z0'=2] {'core','z1',..., dimensions={0} | all-to-all | bytes 2097152 | tf_op jit(solution)/shard_map/all_to_all | solution.py:557
  56.6 1.5 %rows_inverse.1 = f32[4,64,128]{2,1,0:T(8,128)S(1)} custom-call(f32[128,16,128]{2,1,0:T(8,128)S(1)} %all_to_all.11.received, bf16[1536,256]{1,0:T(8,128)(2,1)S(1)} %get-tuple-element.11.tables, f32[160,128]{1,0:T(8,128)S(1)} %get-tuple-element.12.columns), custom_call_target="tpu_custom_call" | custom-call | tf_op jit(solution)/shard_map/rows_inverse/pallas_call | solution.py:504
  58.1 0.1 collective-permute-start.2
  58.2 1.2 %collective-permute-done.2 = f32[2,64,128]{2,1,0:T(8,128)S(1)} collective-permute-done((f32[2,64,128]{2,1,0:T(8,128)S(1)}, f32[2,64,128]{2,1,0:T(8,128)S(1)}, u32[]{:S(2)}, u32[]{:S(2)}) %collective-permute-start.2) | collective-permute-done | bytes 65568 | tf_op jit(solution)/shard_map/ppermute | solution.py:559
  59.4 2.1 %collective-permute-start.4 = (f32[2,64,128]{2,1,0:T(8,128)S(1)}, f32[2,64,128]{2,1,0:T(8,128)S(1)}, u32[]{:S(2)}, u32[]{:S(2)}) collective-permute-start(f32[2,64,128]{2,1,0:T(8,128)S(1)} %pad_maximum_fusion.own), channel_id=1, source_target_pairs={{0,64},{32,96},{64,0},{96,32},{1,65},{33,97},{65,1},{97,33},{2,66}... | collective-permute-start | bytes 196616 | tf_op jit(solution)/shard_map/ppermute | solution.py:564
  61.5 1.6 %collective-permute-start.5 = (f32[2,64,128]{2,1,0:T(8,128)S(1)}, f32[2,64,128]{2,1,0:T(8,128)S(1)}, u32[]{:S(2)}, u32[]{:S(2)}) collective-permute-start(f32[2,64,128]{2,1,0:T(8,128)S(1)} %pad_maximum_fusion.1), channel_id=1, source_target_pairs={{0,96},{32,64},{64,32},{96,0},{1,97},{33,65},{65,33},{97,1},{2,98}... | collective-permute-start | bytes 196616 | tf_op jit(solution)/shard_map/ppermute | solution.py:564
  63.1 0.0 collective-permute-start.3
  63.1 2.2 %collective-permute-done.4.by_grp = f32[2,64,128]{2,1,0:T(8,128)S(1)} collective-permute-done((f32[2,64,128]{2,1,0:T(8,128)S(1)}, f32[2,64,128]{2,1,0:T(8,128)S(1)}, u32[]{:S(2)}, u32[]{:S(2)}) %collective-permute-start.4) | collective-permute-done | bytes 65568 | tf_op jit(solution)/shard_map/ppermute | solution.py:564
  65.3 1.7 %collective-permute-done.5.by_both = f32[2,64,128]{2,1,0:T(8,128)S(1)} collective-permute-done((f32[2,64,128]{2,1,0:T(8,128)S(1)}, f32[2,64,128]{2,1,0:T(8,128)S(1)}, u32[]{:S(2)}, u32[]{:S(2)}) %collective-permute-start.5) | collective-permute-done | bytes 65568 | tf_op jit(solution)/shard_map/ppermute | solution.py:564
  67.0 0.3 collective-permute-done.3.by_row
  67.3 1.0 %assemble.1 = f32[512,128]{1,0:T(8,128)} custom-call(f32[2,64,128]{2,1,0:T(8,128)S(1)} %pad_maximum_fusion.own, f32[2,64,128]{2,1,0:T(8,128)S(1)} %collective-permute-done.3.by_row, f32[2,64,128]{2,1,0:T(8,128)S(1)} %collective-permute-done.4.by_grp, f32[2,64,128]{2,1,0:T(8,128)S(1)} %collective-permute-done.5.by_both), custom_call_target="tpu_custom_call" | custom-call | tf_op jit(solution)/shard_map/assemble/pallas_call | solution.py:516
  (5 shorter events, 0.0 us)
Async XLA Ops:
  0.0 2.4 %collective-permute-start = (f32[512,128]{1,0:T(8,128)}, f32[512,128]{1,0:T(8,128)S(1)}, u32[]{:S(2)}, u32[]{:S(2)}) collective-permute-start(f32[512,128]{1,0:T(8,128)} %bitcast.6), channel_id=1, source_target_pairs={{0,16},{16,0},{1,17},{17,1},{2,18},{18,2},{3,19},{19,3},{4,20},{20... | collective-permute-start | bytes 786440 | tf_op jit(solution)/shard_map/ppermute | solution.py:532
  0.0 2.4 %collective-permute-start.1 = (f32[512,128]{1,0:T(8,128)}, f32[512,128]{1,0:T(8,128)S(1)}, u32[]{:S(2)}, u32[]{:S(2)}) collective-permute-start(f32[512,128]{1,0:T(8,128)} %bitcast.8), channel_id=1, source_target_pairs={{0,16},{16,0},{1,17},{17,1},{2,18},{18,2},{3,19},{19,3},{4,20},{20... | collective-permute-start | bytes 786440 | tf_op jit(solution)/shard_map/ppermute | solution.py:533
  58.1 1.3 %collective-permute-start.2 = (f32[2,64,128]{2,1,0:T(8,128)S(1)}, f32[2,64,128]{2,1,0:T(8,128)S(1)}, u32[]{:S(2)}, u32[]{:S(2)}) collective-permute-start(f32[2,64,128]{2,1,0:T(8,128)S(1)} %slice.21), channel_id=1, source_target_pairs={{0,16},{16,0},{1,17},{17,1},{2,18},{18,2},{3,19},{19,3},{4,20},{20... | collective-permute-start | bytes 196616 | tf_op jit(solution)/shard_map/ppermute | solution.py:559
  59.4 5.9 %collective-permute-start.4 = (f32[2,64,128]{2,1,0:T(8,128)S(1)}, f32[2,64,128]{2,1,0:T(8,128)S(1)}, u32[]{:S(2)}, u32[]{:S(2)}) collective-permute-start(f32[2,64,128]{2,1,0:T(8,128)S(1)} %pad_maximum_fusion.own), channel_id=1, source_target_pairs={{0,64},{32,96},{64,0},{96,32},{1,65},{33,97},{65,1},{97,33},{2,66}... | collective-permute-start | bytes 196616 | tf_op jit(solution)/shard_map/ppermute | solution.py:564
  61.5 5.5 %collective-permute-start.5 = (f32[2,64,128]{2,1,0:T(8,128)S(1)}, f32[2,64,128]{2,1,0:T(8,128)S(1)}, u32[]{:S(2)}, u32[]{:S(2)}) collective-permute-start(f32[2,64,128]{2,1,0:T(8,128)S(1)} %pad_maximum_fusion.1), channel_id=1, source_target_pairs={{0,96},{32,64},{64,32},{96,0},{1,97},{33,65},{65,33},{97,1},{2,98}... | collective-permute-start | bytes 196616 | tf_op jit(solution)/shard_map/ppermute | solution.py:564
  63.1 4.3 %collective-permute-start.3 = (f32[2,64,128]{2,1,0:T(8,128)S(1)}, f32[2,64,128]{2,1,0:T(8,128)S(1)}, u32[]{:S(2)}, u32[]{:S(2)}) collective-permute-start(f32[2,64,128]{2,1,0:T(8,128)S(1)} %pad_maximum_fusion.1), channel_id=1, source_target_pairs={{0,32},{32,0},{64,96},{96,64},{1,33},{33,1},{65,97},{97,65},{2,34}... | collective-permute-start | bytes 196616 | tf_op jit(solution)/shard_map/ppermute | solution.py:564

commit v3 on v2

--- a/solution.py
+++ b/solution.py
@@ -16,6 +16,7 @@
 BF16 = jnp.bfloat16
 C1, C2, C3 = math.cos(math.pi / 8), math.cos(math.pi / 4), math.cos(3 * math.pi / 8)
 LIMIT = 48 * 1024 * 1024
+GROUP = 8
 SCALE = 1.0 / (2048.0 * 2048.0)
 
 
@@ -94,14 +95,14 @@
 def table_times(both, value):
     v_high, v_low = split_value(value)
     rows = both.shape[0] // 2
-    first = mxu(both, v_high)
-    return first[:rows] + (first[rows:] + mxu(both[:rows], v_low))
+    high, low = both[:rows], both[rows:]
+    return mxu(jnp.concatenate([high, high, low], axis=1), jnp.concatenate([v_high, v_low, v_high], axis=0))
 
 
 def times_table(value, both):
     v_high, v_low = split_value(value)
     high, low = both[:256], both[256:]
-    return mxu(v_high, high) + (mxu(v_low, high) + mxu(v_high, low))
+    return mxu(jnp.concatenate([v_high, v_low, v_high], axis=1), jnp.concatenate([high, high, low], axis=0))
 
 
 def fft4(a, b, c, d, sign):
@@ -147,21 +148,10 @@
     return out
 
 
-def swap_blocks(values, lane):
-    values = list(values)
-    low = lane < 64
-    for i in range(4):
-        one, two = values[i], values[i + 4]
-        moved = pltpu.roll(jnp.where(low, two, one), 64, 1)
-        values[i], values[i + 4] = jnp.where(low, one, moved), jnp.where(low, moved, two)
-    for d in (2, 1):
-        low = (lane & (16 * d)) == 0
-        for i in range(8):
-            if i & d:
-                continue
-            one, two = values[i], values[i + d]
-            values[i] = jnp.where(low, one, pltpu.roll(two, 16 * d, 1))
-            values[i + d] = jnp.where(low, pltpu.roll(one, 128 - 16 * d, 1), two)
+def diagonals(values, lane):
+    for d in (1, 2, 4):
+        chosen = (lane & (16 * d)) != 0
+        values = [jnp.where(chosen, values[(i + d) % 8], values[i]) for i in range(8)]
     return values
 
 
@@ -206,11 +196,11 @@
             lanes = pl.ds(128 * (s - 1), 128)
             z_full[rows, lanes] = re * cos + im * sin
             z_full[shifted, lanes] = im * cos - re * sin
-    for pair in range(4):
-        width = 256 if pair < 3 else 128
-        result = table_times(tables[0:512, :], z_full[:, 256 * pair : 256 * pair + width])
-        for k in range(width // 128):
-            at = 256 * (2 * pair + k)
+    for members in ((0,), (1, 2), (3, 4), (5, 6)):
+        lanes = pl.ds(128 * members[0], 128 * len(members))
+        result = table_times(tables[0:512, :], z_full[:, lanes])
+        for k, s in enumerate(members):
+            at = 256 * s
             lanes = slice(128 * k, 128 * k + 128)
             for u in range(8):
                 out[pl.ds(at + 32 * u, 16), :] = result[16 * u : 16 * u + 16, lanes]
@@ -220,7 +210,7 @@
 
 
 def front(members, control, tables, columns, pattern, loc, shell_index, own, tables_v, columns_v, straight, mirrored,
-          pairs_v, loc_v, shells_v, sems):
+          pairs_v, loc_v, shells_v, filters_v, sems):
     core = lax.axis_index("core")
     first = core == 0
     field = pltpu.make_async_copy(members, own, sems.at[0])
@@ -266,35 +256,37 @@
         for shell in range(NSHELL):
             gain = jnp.where(shells == shell, counts[shell : shell + 1, :] * loc_v[:, shell : shell + 1], gain)
         filters.append(gain)
+    for f in range(2 * NBAND):
+        filters_v[f] = filters[f]
     i = lax.broadcasted_iota(jnp.int32, (16, 16), 0)
-    a = lax.broadcasted_iota(jnp.int32, (16, 16), 1)
-    t = 16 * u + i
-    tile = t >> 3
-    negated = jnp.where(s == 0, ((128 - t) & 127) >> 3, 15 - tile)
-    pick = (a == tile, a == negated)
-    swap_row = jnp.logical_and(special, i == 0)
-    partner = tuple(a == jnp.where(swap_row, 8, chosen) for chosen in (tile, negated))
-    lane = lax.broadcasted_iota(jnp.int32, (16, 128), 1)
-    tile_row = lax.broadcasted_iota(jnp.int32, (16, 128), 0)
-    spread = tile_row == (lane >> 3)
-    spread_neg = (tile_row == (((128 - lane) & 127) >> 3), tile_row == 15 - (lane >> 3))
-
-    def as_f32(mask):
-        return jnp.where(mask, 1.0, 0.0).astype(F32)
-
-    def dot(x, y):
-        return jnp.dot(x, y, preferred_element_type=F32, precision=lax.Precision.HIGHEST)
-
-    choose = jnp.concatenate([as_f32(m) for m in pick + partner], axis=0)
-    widen = jnp.concatenate([as_f32(m) for m in (spread,) + spread_neg], axis=1)
+    picked = []
     for f in range(2 * NBAND):
-        wide = dot(dot(choose, filters[f]), widen)
+
+        def tile_row(tile):
+            return filters_v[f, pl.ds(tile, 1), :]
+
+        here = jnp.where(i < 8, tile_row(2 * u), tile_row(2 * u + 1))
+        negated = jnp.where(i < jnp.where(s == 0, 9, 8), tile_row(15 - 2 * u), tile_row(14 - 2 * u))
+        negated = jnp.where(jnp.logical_and(i == 0, s == 0), tile_row((16 - 2 * u) & 15), negated)
+        picked += [here, negated, jnp.broadcast_to(tile_row(8), (8, 16))]
+    picked = jnp.concatenate(picked, axis=0)
+    high, rest = split_value(picked)
+    middle = (picked - high.astype(F32) - rest.astype(F32)).astype(BF16)
+    tile = lax.broadcasted_iota(jnp.int32, (48, 128), 0) & 15
+    lane = lax.broadcasted_iota(jnp.int32, (48, 128), 1)
+    spread = [tile == (lane >> 3), tile == (((128 - lane) & 127) >> 3), tile == 15 - (lane >> 3)]
+    widen = jnp.concatenate([jnp.where(mask, 1.0, 0.0).astype(BF16) for mask in spread], axis=1)
+    wide = mxu(jnp.concatenate([high, rest, middle], axis=1), widen)
+    first_row = jnp.logical_and(special, lax.broadcasted_iota(jnp.int32, (8, 128), 0) == 0)
+    for f in range(2 * NBAND):
         for kind in range(2):
             at = slice(128 + 128 * kind, 256 + 128 * kind)
-            here = 0.5 * (wide[0:16, :128] + wide[16:32, at])
-            other = 0.5 * (wide[32:48, :128] + wide[48:64, at])
-            straight[kind, f] = 0.5 * (here + other)
-            mirrored[kind, f] = (0.5 * (here - other))[0:8]
+            top = 40 * f
+            gain = 0.5 * (wide[top : top + 16, :128] + wide[top + 16 : top + 32, at])
+            other = 0.5 * (wide[top + 32 : top + 40, :128] + wide[top + 32 : top + 40, at])
+            straight[kind, f, 0:8] = jnp.where(first_row, 0.5 * (gain[0:8] + other), gain[0:8])
+            straight[kind, f, 8:16] = gain[8:16]
+            mirrored[kind, f] = jnp.where(first_row, 0.5 * (gain[0:8] - other), 0.0)
     field.wait()
     for copy in large:
         copy.wait()
@@ -308,82 +300,103 @@
         z[s, field, at, 0:128] = zr * wr - zi * wi
         z[s, field, at, 128:256] = zr * wi + zi * wr
 
-    for field in range(2):
-        for half in range(2):
-            re_at, im_at = pl.ds(8 * half, 8), pl.ds(16 + 8 * half, 8)
-            values = []
-            for c in range(16):
-                one, two = [place_of(FIRST, {"ylo": ylo, "core": field, **block_at(c)}) for ylo in range(2)]
-                values.append(
-                    (received[one, re_at, :] + received[two, re_at, :], received[one, im_at, :] + received[two, im_at, :])
-                )
-            values = fft16(values, -1)
-            for s in range(16):
-                put(s, field, re_at, *values[s])
-                if half == 0:
-                    mr, mi = values[(16 - s) % 16]
-                    put(s, field, pl.ds(16, 8), mr, -mi)
-    for group in range(4):
-        spectrum = times_table(z[pl.ds(4 * group, 4)].reshape(4 * 2 * 24, 256), tables[512:1024, :])
-        spectrum = spectrum.reshape(4, 2, 24, 256)
+    lane = lax.broadcasted_iota(jnp.int32, (8, 128), 1)
+    grp = lax.axis_index("grp")
+    shifts = [(16 * (e + grp)) & 127 for e in range(8)]
+
+    def forward(field, half):
+        re_at, im_at = pl.ds(8 * half, 8), pl.ds(16 + 8 * half, 8)
+        values = []
+        for c in range(16):
+            one, two = [place_of(FIRST, {"ylo": ylo, "core": field, **block_at(c)}) for ylo in range(2)]
+            values.append(
+                (received[one, re_at, :] + received[two, re_at, :], received[one, im_at, :] + received[two, im_at, :])
+            )
+        values = fft16(values, -1)
+        for s in range(16):
+            put(s, field, re_at, *values[s])
+            if half == 0:
+                mr, mi = values[(16 - s) % 16]
+                put(s, field, pl.ds(16, 8), mr, -mi)
+
+    def spectral(field, group):
+        steps = range(GROUP * group, GROUP * group + GROUP)
+        spectrum = times_table(z[pl.ds(steps[0], GROUP), field].reshape(GROUP * 24, 256), tables[512:1024, :])
+        spectrum = spectrum.reshape(GROUP, 24, 256)
         filtered = []
-        for step in range(4):
-            kind = 0 if group == 0 and step == 0 else 1
-            for f in range(4):
-                tile = spectrum[step, f // 2]
+        for step in range(GROUP):
+            kind = 0 if steps[step] == 0 else 1
+            tile = spectrum[step]
+            for f in (2 * field, 2 * field + 1):
                 gain = straight[kind, f]
                 mirror = mirrored[kind, f]
                 gain = jnp.concatenate([gain, gain], axis=1)
                 mirror = jnp.concatenate([mirror, mirror], axis=1)
                 top = gain[0:8] * tile[0:8] + mirror * tile[16:24]
                 filtered.append(jnp.concatenate([top, gain[8:16] * tile[8:16]], axis=0))
-        filtered = jnp.concatenate(filtered, axis=0)
-        back = times_table(filtered, tables[0:512, :])
-        y[pl.ds(4 * group, 4)] = back.reshape(4, 4, 16, 256)
-    lane = lax.broadcasted_iota(jnp.int32, (8, 128), 1)
-    for half in range(2):
+        back = times_table(jnp.concatenate(filtered, axis=0), tables[0:512, :])
+        y[pl.ds(steps[0], GROUP), pl.ds(2 * field, 2)] = back.reshape(GROUP, 2, 16, 256)
+
+    def inverse(f, half):
         at = pl.ds(8 * half, 8)
-        for f in range(4):
-            values = []
-            for s in range(16):
-                re, im = y[s, f, at, 0:128], y[s, f, at, 128:256]
-                wr, wi = tw[s]
-                values.append((re * wr + im * wi, im * wr - re * wi))
-            values = fft16(values, 1)
-            for c in range(16):
-                v[f, c, 0] = values[c][0]
-                v[f, c, 1] = values[c][1]
+        values = []
+        for s in range(16):
+            re, im = y[s, f, at, 0:128], y[s, f, at, 128:256]
+            wr, wi = tw[s]
+            values.append((re * wr + im * wi, im * wr - re * wi))
+        values = fft16(values, 1)
         for c in range(16):
-            moved = swap_blocks([v[f, c, part] for f in range(4) for part in range(2)], lane)
-            for q in range(8):
-                target = {"grp": q >> 2, "ylo": (q >> 1) & 1, "core": q & 1, **block_at(c)}
-                out[place_of(SECOND, target), at, :] = moved[q]
+            v[f, c, 0, at] = values[c][0]
+            v[f, c, 1, at] = values[c][1]
+
+    def send(half, c):
+        at = pl.ds(8 * half, 8)
+        turned = [pltpu.roll(v[e >> 1, c, e & 1, at], shifts[e], 1) for e in range(8)]
+        for i, moved in enumerate(diagonals(turned, lane)):
+            q = (-i - grp) & 7
+            target = {"grp": q >> 2, "ylo": (q >> 1) & 1, "core": q & 1, **block_at(c)}
+            out[place_of(SECOND, target), at, :] = moved
+
+    forward(0, 0)
+    forward(0, 1)
+    for group in range(16 // GROUP):
+        spectral(0, group)
+    forward(1, 0)
+    forward(1, 1)
+    for group in range(16 // GROUP):
+        spectral(1, group)
+    for f, half in ((0, 0), (1, 0), (0, 1), (1, 1), (2, 0), (3, 0)):
+        inverse(f, half)
+    for c in range(16):
+        send(0, c)
+    inverse(2, 1)
+    inverse(3, 1)
+    for c in range(16):
+        send(1, c)
 
 
 def rows_inverse(received, tables, columns, out, z_full, z_half):
     row = lax.axis_index("ylo") * 2 + lax.axis_index("core")
-    lane16 = lax.broadcasted_iota(jnp.int32, (16, 128), 1)
-    even = (lane16 & 16) == 0
+    mine = lax.axis_index("grp") * 4 + row
+    even = ((lax.broadcasted_iota(jnp.int32, (16, 128), 1) - 16 * mine) & 16) == 0
 
     def chunk(d):
         one, two = received[of_group(0, d)], received[of_group(1, d)]
-        re = jnp.where(even, one, pltpu.roll(two, 16, 1))
-        im = jnp.where(even, pltpu.roll(one, 112, 1), two)
-        return re, im
-
-    for pair in range(4):
+        return jnp.where(even, one, two), pltpu.roll(jnp.where(even, two, one), 112, 1)
+
+    for members in ((0,), (1, 2), (3, 4), (5, 6)):
         spectra = []
-        for s in range(2 * pair, min(2 * pair + 2, 7)):
+        for s in members:
             parts = [chunk(8 * s + u) for u in range(8)]
             spectra.append(jnp.concatenate([p[0] for p in parts] + [p[1] for p in parts], axis=0))
-        result = table_times(tables[512:1024, :], jnp.concatenate(spectra, axis=1) if len(spectra) > 1 else spectra[0])
-        for k in range(len(spectra)):
-            z_full[2 * pair + k] = result[:, 128 * k : 128 * k + 128]
+        result = table_times(tables[512:1024, :], jnp.concatenate(spectra, axis=1))
+        for k, s in enumerate(members):
+            z_full[s] = result[:, 128 * k : 128 * k + 128]
     for s in range(2):
         parts = [chunk(56 + 4 * s + u) for u in range(4)]
         z_half[s] = table_times(tables[1280:1536, 128 * s : 128 * s + 128], jnp.concatenate([p[k] for p in parts for k in range(2)], axis=0))
-    lane = lax.broadcasted_iota(jnp.int32, (8, 128), 1)
-    low64, low32, low16 = lane < 64, (lane & 32) == 0, (lane & 16) == 0
+    lane = lax.broadcasted_iota(jnp.int32, (8, 128), 1) - 16 * mine
+    low64, low32, low16 = (lane & 64) == 0, (lane & 32) == 0, (lane & 16) == 0
 
     def fold(one, two, low, shift):
         other = jnp.where(low, two, one)
@@ -431,16 +444,24 @@
     return x
 
 
-def assemble(own, by_row, by_grp, by_both, out, pieces):
+def assemble(own, by_row, by_grp, by_both, out, pieces, whole, sems):
     mine = (lax.axis_index("grp") * 2 + lax.axis_index("ylo")) * 2 + lax.axis_index("core")
     for k, ref in enumerate((own, by_row, by_grp, by_both)):
         pieces[pl.ds(2 * k, 2)] = ref[...]
     lane = lax.broadcasted_iota(jnp.int32, (8, 128), 1)
-    for slab in range(8):
-        rows = pl.ds(slab * 8, 8)
-        moved = swap_blocks([pieces[q ^ mine, rows, :] for q in range(8)], lane)
-        for e in range(8):
-            out[pl.ds(128 * (e & 3) + 64 * (e >> 2) + slab * 8, 8), :] = moved[e]
+    copies = []
+    for part in range(2):
+        for slab in range(4 * part, 4 * part + 4):
+            rows = pl.ds(slab * 8, 8)
+            for i, moved in enumerate(diagonals([pieces[q ^ mine, rows, :] for q in range(8)], lane)):
+                e = -i % 8
+                whole[e & 3, e >> 2, rows, :] = pltpu.roll(moved, 16 * i, 1) if i else moved
+        rows = pl.ds(32 * part, 32)
+        copy = pltpu.make_async_copy(whole.at[:, :, rows, :], out.at[:, :, rows, :], sems.at[part])
+        copy.start()
+        copies.append(copy)
+    for copy in copies:
+        copy.wait()
 
 
 def in_vmem(count):
@@ -493,7 +514,7 @@
         scratch_shapes=[
             pltpu.VMEM((16, 2, 24, 256), F32),
             pltpu.VMEM((16, 4, 16, 256), F32),
-            pltpu.VMEM((4, 16, 2, 8, 128), F32),
+            pltpu.VMEM((4, 16, 2, 16, 128), F32),
         ],
         compiler_params=params(),
         name="cols_filter",
@@ -515,23 +536,21 @@
 def call_assemble(near, by_row, by_grp, by_both):
     return pl.pallas_call(
         assemble,
-        out_shape=shape(512, 128),
+        out_shape=shape(4, 2, 64, 128),
         in_specs=in_vmem(4),
-        out_specs=in_vmem(1)[0],
-        scratch_shapes=[pltpu.VMEM((8, 64, 128), F32)],
+        out_specs=pl.BlockSpec(memory_space=pltpu.HBM),
+        scratch_shapes=[
+            pltpu.VMEM((8, 64, 128), F32),
+            pltpu.VMEM((4, 2, 64, 128), F32),
+            pltpu.SemaphoreType.DMA((2,)),
+        ],
         compiler_params=params(),
         name="assemble",
-    )(near, by_row, by_grp, by_both)
-
-
-def on_device(members, control, loc_spectrum, pattern, shell_index):
-    tables, columns = constant_tables()
-    members = members.reshape(512, 128)
-    control = control.reshape(512, 128)
-    swap_cores = [(0, 1), (1, 0)]
-    got_members = lax.ppermute(members, "core", swap_cores)
-    got_control = lax.ppermute(control, "core", swap_cores)
-    own, tables, columns, straight, mirrored = pl.pallas_call(
+    )(near, by_row, by_grp, by_both).reshape(512, 128)
+
+
+def call_front(members, control, tables, columns, pattern, loc_spectrum, shell_index):
+    return pl.pallas_call(
         front,
         out_shape=(
             shape(512, 128),
@@ -546,11 +565,24 @@
             pltpu.VMEM((2, pattern.shape[0]), jnp.int32),
             pltpu.VMEM((1, NSHELL), F32),
             pltpu.VMEM(shell_index.shape, jnp.int32),
+            pltpu.VMEM((2 * NBAND, *shell_index.shape), F32),
             pltpu.SemaphoreType.DMA((6,)),
         ],
         compiler_params=params(),
         name="front",
     )(*in_hbm(members, control, tables, columns, pattern.T, loc_spectrum.reshape(1, NSHELL), shell_index))
+
+
+def on_device(members, control, loc_spectrum, pattern, shell_index):
+    tables, columns = constant_tables()
+    members = members.reshape(512, 128)
+    control = control.reshape(512, 128)
+    swap_cores = [(0, 1), (1, 0)]
+    got_members = lax.ppermute(members, "core", swap_cores)
+    got_control = lax.ppermute(control, "core", swap_cores)
+    own, tables, columns, straight, mirrored = call_front(
+        members, control, tables, columns, pattern, loc_spectrum, shell_index
+    )
     spectra = call_rows_forward(own, got_members, got_control, tables, columns)
     spectra = lax.all_to_all(spectra.reshape(64, 32, 128), FIRST, split_axis=0, concat_axis=0, tiled=True)
     filtered = call_cols_filter(spectra, straight, mirrored, tables, columns)

time: 68.5 us -> 67.2 us (0.981)
  Pallas kernels: 7.37 us -> 5.73 us
    pallas_call x2, Pallas kernels: 2.9 us -> 2.15 us  [the longest x1 1.31 us: call_front(): pl.pallas_call(front, out_shape=(shape(512, 128), jax.ShapeDtypeStruct(ta...]
  transfers between devices with their start and end apart: 6 -> 6, of which waited for: 4 -> 5; matrix products, arithmetic and copies ran while one was open for 0% -> 0% of each run, Pallas kernels for 3% -> 2%
where the time goes in v3:
time: 67.2 us; the launch traced here: 67 us
  blocking collectives  51.2 us (76%)
  waiting for transfers between devices  5.77 us (9%)
  Pallas kernels  5.73 us (9%)
  starting transfers between devices  4.21 us (6%)
    all_to_all x1, blocking collectives, on_device(): lax.all_to_all(spectra.reshape(64, 32, 128), FIRST, split_axis=0, concat_...  26.5 us
    all_to_all x1, blocking collectives, on_device(): lax.all_to_all(filtered, SECOND, split_axis=0, concat_axis=0, tiled=True)  24.6 us
    ppermute x3, waiting for transfers between devices, exchange(): lax.ppermute(value, ('grp', 'ylo'), [(i, i ^ step) for i in range(4)])  4.26 us
    ppermute x3, starting transfers between devices, exchange(): lax.ppermute(value, ('grp', 'ylo'), [(i, i ^ step) for i in range(4)])  3.62 us
    pallas_call x1, Pallas kernels, call_cols_filter(): pl.pallas_call(cols_filter, out_shape=shape(128, 16, 128), in_specs=in_vm...  1.53 us
  transfers between devices with their start and end apart: 6, of which 5 were waited for; matrix products, arithmetic and copies ran while one was open for 0% of the time, Pallas kernels for 2%

profile of v3, /device:TPU:0, one launch (start us, length us, event | category | flops | bytes accessed | tf_op | source)
XLA Modules:
  0.0 67.0 jit_solution(8593813835696068227)
XLA Ops:
  0.0 0.0 collective-permute-start
  0.0 0.5 collective-permute-start.1
  0.5 1.3 %front.1 = (f32[512,128]{1,0:T(8,128)S(1)}, bf16[1536,256]{1,0:T(8,128)(2,1)S(1)}, f32[160,128]{1,0:T(8,128)S(1)}, f32[2,4,16,128]{3,2,1,0:T(8,128)S(1)}, f32[2,4,8,128]{3,2,1,0:T(8,128)S(1)}) custom-call(f32[512,128]{1,0:T(8,128)} %bitcast.8, f32[512,128]{1,0:T(8,128)} %bitcast.10, bf16[1536,256]{1,0:T(8,128)(2,1)} %constant.4.clone.tables, ...), custom_call_target="tpu_custom_call" | custom-call | tf_op jit(solution)/shard_map/front/pallas_call | solution.py:553
  1.8 0.0 collective-permute-done.got_members
  1.8 0.3 collective-permute-done.1.got_control
  2.1 0.8 %rows_forward.1 = f32[2048,128]{1,0:T(8,128)S(1)} custom-call(f32[512,128]{1,0:T(8,128)S(1)} %get-tuple-element.10.own, f32[512,128]{1,0:T(8,128)S(1)} %collective-permute-done.got_members, f32[512,128]{1,0:T(8,128)S(1)} %collective-permute-done.1.got_control, bf16[1536,256]{1,0:T(8,128)(2,1)S(1)} %get-tuple-element.11.tables, ...), custom_call_target="tpu_custom_call" | custom-call | tf_op jit(solution)/shard_map/rows_forward/pallas_call | solution.py:497
  3.0 26.5 %all_to_all.10.received = f32[64,32,128]{2,1,0:T(8,128)S(1)} all-to-all(f32[64,32,128]{2,1,0:T(8,128)S(1)} %bitcast.6), channel_id=1, replica_groups=mesh['grp'=2,'ylo'=2,'core'=2,'x1'=2,'x0'=2,'z1'=2,'z0'=2] {'x1','x0','c..., dimensions={0} | all-to-all | bytes 2097152 | tf_op jit(solution)/shard_map/all_to_all | solution.py:587
  29.5 1.5 %cols_filter.1 = f32[128,16,128]{2,1,0:T(8,128)S(1)} custom-call(f32[64,32,128]{2,1,0:T(8,128)S(1)} %all_to_all.10.received, f32[2,4,16,128]{3,2,1,0:T(8,128)S(1)} %get-tuple-element.13.straight, f32[2,4,8,128]{3,2,1,0:T(8,128)S(1)} %get-tuple-element.14.mirrored, bf16[1536,256]{1,0:T(8,128)(2,1)S(1)} %get-tuple-element.11.tables, ...), custom_call_target="tpu_custom_call" | custom-call | tf_op jit(solution)/shard_map/cols_filter/pallas_call | solution.py:509
  31.0 24.6 %all_to_all.11.received = f32[128,16,128]{2,1,0:T(8,128)S(1)} all-to-all(f32[128,16,128]{2,1,0:T(8,128)S(1)} %cols_filter.1), channel_id=1, replica_groups=mesh['grp'=2,'ylo'=2,'core'=2,'x1'=2,'x0'=2,'z1'=2,'z0'=2] {'core','z1',..., dimensions={0} | all-to-all | bytes 2097152 | tf_op jit(solution)/shard_map/all_to_all | solution.py:589
  55.7 1.2 %rows_inverse.1 = f32[4,64,128]{2,1,0:T(8,128)S(1)} custom-call(f32[128,16,128]{2,1,0:T(8,128)S(1)} %all_to_all.11.received, bf16[1536,256]{1,0:T(8,128)(2,1)S(1)} %get-tuple-element.11.tables, f32[160,128]{1,0:T(8,128)S(1)} %get-tuple-element.12.columns), custom_call_target="tpu_custom_call" | custom-call | tf_op jit(solution)/shard_map/rows_inverse/pallas_call | solution.py:525
  56.9 0.1 collective-permute-start.2
  57.0 1.2 %collective-permute-done.2 = f32[2,64,128]{2,1,0:T(8,128)S(1)} collective-permute-done((f32[2,64,128]{2,1,0:T(8,128)S(1)}, f32[2,64,128]{2,1,0:T(8,128)S(1)}, u32[]{:S(2)}, u32[]{:S(2)}) %collective-permute-start.2) | collective-permute-done | bytes 65568 | tf_op jit(solution)/shard_map/ppermute | solution.py:591
  58.2 2.1 %collective-permute-start.4 = (f32[2,64,128]{2,1,0:T(8,128)S(1)}, f32[2,64,128]{2,1,0:T(8,128)S(1)}, u32[]{:S(2)}, u32[]{:S(2)}) collective-permute-start(f32[2,64,128]{2,1,0:T(8,128)S(1)} %pad_maximum_fusion.own), channel_id=1, source_target_pairs={{0,64},{32,96},{64,0},{96,32},{1,65},{33,97},{65,1},{97,33},{2,66}... | collective-permute-start | bytes 196616 | tf_op jit(solution)/shard_map/ppermute | solution.py:596
  60.3 1.6 %collective-permute-start.5 = (f32[2,64,128]{2,1,0:T(8,128)S(1)}, f32[2,64,128]{2,1,0:T(8,128)S(1)}, u32[]{:S(2)}, u32[]{:S(2)}) collective-permute-start(f32[2,64,128]{2,1,0:T(8,128)S(1)} %pad_maximum_fusion.1), channel_id=1, source_target_pairs={{0,96},{32,64},{64,32},{96,0},{1,97},{33,65},{65,33},{97,1},{2,98}... | collective-permute-start | bytes 196616 | tf_op jit(solution)/shard_map/ppermute | solution.py:596
  61.9 0.0 collective-permute-start.3
  61.9 2.2 %collective-permute-done.4.by_grp = f32[2,64,128]{2,1,0:T(8,128)S(1)} collective-permute-done((f32[2,64,128]{2,1,0:T(8,128)S(1)}, f32[2,64,128]{2,1,0:T(8,128)S(1)}, u32[]{:S(2)}, u32[]{:S(2)}) %collective-permute-start.4) | collective-permute-done | bytes 65568 | tf_op jit(solution)/shard_map/ppermute | solution.py:596
  64.1 1.7 %collective-permute-done.5.by_both = f32[2,64,128]{2,1,0:T(8,128)S(1)} collective-permute-done((f32[2,64,128]{2,1,0:T(8,128)S(1)}, f32[2,64,128]{2,1,0:T(8,128)S(1)}, u32[]{:S(2)}, u32[]{:S(2)}) %collective-permute-start.5) | collective-permute-done | bytes 65568 | tf_op jit(solution)/shard_map/ppermute | solution.py:596
  65.8 0.3 collective-permute-done.3.by_row
  66.1 0.8 %assemble.1 = f32[4,2,64,128]{3,2,1,0:T(8,128)} custom-call(f32[2,64,128]{2,1,0:T(8,128)S(1)} %pad_maximum_fusion.own, f32[2,64,128]{2,1,0:T(8,128)S(1)} %collective-permute-done.3.by_row, f32[2,64,128]{2,1,0:T(8,128)S(1)} %collective-permute-done.4.by_grp, f32[2,64,128]{2,1,0:T(8,128)S(1)} %collective-permute-done.5.by_both), custom_call_target="tpu_custom_call" | custom-call | tf_op jit(solution)/shard_map/assemble/pallas_call | solution.py:537
  (5 shorter events, 0.0 us)
Async XLA Ops:
  0.0 1.8 %collective-permute-start = (f32[512,128]{1,0:T(8,128)}, f32[512,128]{1,0:T(8,128)S(1)}, u32[]{:S(2)}, u32[]{:S(2)}) collective-permute-start(f32[512,128]{1,0:T(8,128)} %bitcast.7), channel_id=1, source_target_pairs={{0,16},{16,0},{1,17},{17,1},{2,18},{18,2},{3,19},{19,3},{4,20},{20... | collective-permute-start | bytes 786440 | tf_op jit(solution)/shard_map/ppermute | solution.py:581
  0.0 2.1 %collective-permute-start.1 = (f32[512,128]{1,0:T(8,128)}, f32[512,128]{1,0:T(8,128)S(1)}, u32[]{:S(2)}, u32[]{:S(2)}) collective-permute-start(f32[512,128]{1,0:T(8,128)} %bitcast.9), channel_id=1, source_target_pairs={{0,16},{16,0},{1,17},{17,1},{2,18},{18,2},{3,19},{19,3},{4,20},{20... | collective-permute-start | bytes 786440 | tf_op jit(solution)/shard_map/ppermute | solution.py:582
  56.9 1.3 %collective-permute-start.2 = (f32[2,64,128]{2,1,0:T(8,128)S(1)}, f32[2,64,128]{2,1,0:T(8,128)S(1)}, u32[]{:S(2)}, u32[]{:S(2)}) collective-permute-start(f32[2,64,128]{2,1,0:T(8,128)S(1)} %slice.21), channel_id=1, source_target_pairs={{0,16},{16,0},{1,17},{17,1},{2,18},{18,2},{3,19},{19,3},{4,20},{20... | collective-permute-start | bytes 196616 | tf_op jit(solution)/shard_map/ppermute | solution.py:591
  58.2 5.9 %collective-permute-start.4 = (f32[2,64,128]{2,1,0:T(8,128)S(1)}, f32[2,64,128]{2,1,0:T(8,128)S(1)}, u32[]{:S(2)}, u32[]{:S(2)}) collective-permute-start(f32[2,64,128]{2,1,0:T(8,128)S(1)} %pad_maximum_fusion.own), channel_id=1, source_target_pairs={{0,64},{32,96},{64,0},{96,32},{1,65},{33,97},{65,1},{97,33},{2,66}... | collective-permute-start | bytes 196616 | tf_op jit(solution)/shard_map/ppermute | solution.py:596
  60.3 5.5 %collective-permute-start.5 = (f32[2,64,128]{2,1,0:T(8,128)S(1)}, f32[2,64,128]{2,1,0:T(8,128)S(1)}, u32[]{:S(2)}, u32[]{:S(2)}) collective-permute-start(f32[2,64,128]{2,1,0:T(8,128)S(1)} %pad_maximum_fusion.1), channel_id=1, source_target_pairs={{0,96},{32,64},{64,32},{96,0},{1,97},{33,65},{65,33},{97,1},{2,98}... | collective-permute-start | bytes 196616 | tf_op jit(solution)/shard_map/ppermute | solution.py:596
  61.9 4.3 %collective-permute-start.3 = (f32[2,64,128]{2,1,0:T(8,128)S(1)}, f32[2,64,128]{2,1,0:T(8,128)S(1)}, u32[]{:S(2)}, u32[]{:S(2)}) collective-permute-start(f32[2,64,128]{2,1,0:T(8,128)S(1)} %pad_maximum_fusion.1), channel_id=1, source_target_pairs={{0,32},{32,0},{64,96},{96,64},{1,33},{33,1},{65,97},{97,65},{2,34}... | collective-permute-start | bytes 196616 | tf_op jit(solution)/shard_map/ppermute | solution.py:596

commit v4 on v3

--- a/solution.py
+++ b/solution.py
@@ -16,7 +16,7 @@
 BF16 = jnp.bfloat16
 C1, C2, C3 = math.cos(math.pi / 8), math.cos(math.pi / 4), math.cos(3 * math.pi / 8)
 LIMIT = 48 * 1024 * 1024
-GROUP = 8
+GROUP = 16
 SCALE = 1.0 / (2048.0 * 2048.0)
 
 
@@ -320,22 +320,22 @@
                 put(s, field, pl.ds(16, 8), mr, -mi)
 
     def spectral(field, group):
-        steps = range(GROUP * group, GROUP * group + GROUP)
-        spectrum = times_table(z[pl.ds(steps[0], GROUP), field].reshape(GROUP * 24, 256), tables[512:1024, :])
-        spectrum = spectrum.reshape(GROUP, 24, 256)
-        filtered = []
-        for step in range(GROUP):
-            kind = 0 if steps[step] == 0 else 1
-            tile = spectrum[step]
-            for f in (2 * field, 2 * field + 1):
+        steps = range(16 * group, 16 * group + 16)
+        spectrum = times_table(z[pl.ds(steps[0], 16), field].reshape(16 * 24, 256), tables[512:1024, :])
+        spectrum = spectrum.reshape(16, 24, 256)
+        for f in (2 * field, 2 * field + 1):
+            filtered = []
+            for step in range(16):
+                kind = 0 if steps[step] == 0 else 1
+                tile = spectrum[step]
                 gain = straight[kind, f]
                 mirror = mirrored[kind, f]
                 gain = jnp.concatenate([gain, gain], axis=1)
                 mirror = jnp.concatenate([mirror, mirror], axis=1)
                 top = gain[0:8] * tile[0:8] + mirror * tile[16:24]
                 filtered.append(jnp.concatenate([top, gain[8:16] * tile[8:16]], axis=0))
-        back = times_table(jnp.concatenate(filtered, axis=0), tables[0:512, :])
-        y[pl.ds(steps[0], GROUP), pl.ds(2 * field, 2)] = back.reshape(GROUP, 2, 16, 256)
+            back = times_table(jnp.concatenate(filtered, axis=0), tables[0:512, :])
+            y[pl.ds(steps[0], 16), f] = back.reshape(16, 16, 256)
 
     def inverse(f, half):
         at = pl.ds(8 * half, 8)

time: 67.2 us -> 67 us (level)
  no operation moved by 1% of the time
where the time goes in v4:
time: 67 us; the launch traced here: 66.8 us
  blocking collectives  51.2 us (76%)
  waiting for transfers between devices  5.77 us (9%)
  Pallas kernels  5.58 us (8%)
  starting transfers between devices  4.22 us (6%)
    all_to_all x1, blocking collectives, on_device(): lax.all_to_all(spectra.reshape(64, 32, 128), FIRST, split_axis=0, concat_...  26.5 us
    all_to_all x1, blocking collectives, on_device(): lax.all_to_all(filtered, SECOND, split_axis=0, concat_axis=0, tiled=True)  24.6 us
    ppermute x3, waiting for transfers between devices, exchange(): lax.ppermute(value, ('grp', 'ylo'), [(i, i ^ step) for i in range(4)])  4.26 us
    ppermute x3, starting transfers between devices, exchange(): lax.ppermute(value, ('grp', 'ylo'), [(i, i ^ step) for i in range(4)])  3.63 us
    pallas_call x1, Pallas kernels, call_cols_filter(): pl.pallas_call(cols_filter, out_shape=shape(128, 16, 128), in_specs=in_vm...  1.38 us
  transfers between devices with their start and end apart: 6, of which 5 were waited for; matrix products, arithmetic and copies ran while one was open for 0% of the time, Pallas kernels for 2%

profile of v4, /device:TPU:0, one launch (start us, length us, event | category | flops | bytes accessed | tf_op | source)
XLA Modules:
  0.0 66.8 jit_solution(15421975916766588161)
XLA Ops:
  0.0 0.0 collective-permute-start
  0.0 0.5 collective-permute-start.1
  0.5 1.3 %front.1 = (f32[512,128]{1,0:T(8,128)S(1)}, bf16[1536,256]{1,0:T(8,128)(2,1)S(1)}, f32[160,128]{1,0:T(8,128)S(1)}, f32[2,4,16,128]{3,2,1,0:T(8,128)S(1)}, f32[2,4,8,128]{3,2,1,0:T(8,128)S(1)}) custom-call(f32[512,128]{1,0:T(8,128)} %bitcast.8, f32[512,128]{1,0:T(8,128)} %bitcast.10, bf16[1536,256]{1,0:T(8,128)(2,1)} %constant.4.clone.tables, ...), custom_call_target="tpu_custom_call" | custom-call | tf_op jit(solution)/shard_map/front/pallas_call | solution.py:553
  1.8 0.0 collective-permute-done.got_members
  1.8 0.3 collective-permute-done.1.got_control
  2.1 0.8 %rows_forward.1 = f32[2048,128]{1,0:T(8,128)S(1)} custom-call(f32[512,128]{1,0:T(8,128)S(1)} %get-tuple-element.10.own, f32[512,128]{1,0:T(8,128)S(1)} %collective-permute-done.got_members, f32[512,128]{1,0:T(8,128)S(1)} %collective-permute-done.1.got_control, bf16[1536,256]{1,0:T(8,128)(2,1)S(1)} %get-tuple-element.11.tables, ...), custom_call_target="tpu_custom_call" | custom-call | tf_op jit(solution)/shard_map/rows_forward/pallas_call | solution.py:497
  3.0 26.5 %all_to_all.10.received = f32[64,32,128]{2,1,0:T(8,128)S(1)} all-to-all(f32[64,32,128]{2,1,0:T(8,128)S(1)} %bitcast.6), channel_id=1, replica_groups=mesh['grp'=2,'ylo'=2,'core'=2,'x1'=2,'x0'=2,'z1'=2,'z0'=2] {'x1','x0','c..., dimensions={0} | all-to-all | bytes 2097152 | tf_op jit(solution)/shard_map/all_to_all | solution.py:587
  29.5 1.4 %cols_filter.1 = f32[128,16,128]{2,1,0:T(8,128)S(1)} custom-call(f32[64,32,128]{2,1,0:T(8,128)S(1)} %all_to_all.10.received, f32[2,4,16,128]{3,2,1,0:T(8,128)S(1)} %get-tuple-element.13.straight, f32[2,4,8,128]{3,2,1,0:T(8,128)S(1)} %get-tuple-element.14.mirrored, bf16[1536,256]{1,0:T(8,128)(2,1)S(1)} %get-tuple-element.11.tables, ...), custom_call_target="tpu_custom_call" | custom-call | tf_op jit(solution)/shard_map/cols_filter/pallas_call | solution.py:509
  30.9 24.6 %all_to_all.11.received = f32[128,16,128]{2,1,0:T(8,128)S(1)} all-to-all(f32[128,16,128]{2,1,0:T(8,128)S(1)} %cols_filter.1), channel_id=1, replica_groups=mesh['grp'=2,'ylo'=2,'core'=2,'x1'=2,'x0'=2,'z1'=2,'z0'=2] {'core','z1',..., dimensions={0} | all-to-all | bytes 2097152 | tf_op jit(solution)/shard_map/all_to_all | solution.py:589
  55.5 1.2 %rows_inverse.1 = f32[4,64,128]{2,1,0:T(8,128)S(1)} custom-call(f32[128,16,128]{2,1,0:T(8,128)S(1)} %all_to_all.11.received, bf16[1536,256]{1,0:T(8,128)(2,1)S(1)} %get-tuple-element.11.tables, f32[160,128]{1,0:T(8,128)S(1)} %get-tuple-element.12.columns), custom_call_target="tpu_custom_call" | custom-call | tf_op jit(solution)/shard_map/rows_inverse/pallas_call | solution.py:525
  56.7 0.1 collective-permute-start.2
  56.9 1.2 %collective-permute-done.2 = f32[2,64,128]{2,1,0:T(8,128)S(1)} collective-permute-done((f32[2,64,128]{2,1,0:T(8,128)S(1)}, f32[2,64,128]{2,1,0:T(8,128)S(1)}, u32[]{:S(2)}, u32[]{:S(2)}) %collective-permute-start.2) | collective-permute-done | bytes 65568 | tf_op jit(solution)/shard_map/ppermute | solution.py:591
  58.1 2.1 %collective-permute-start.4 = (f32[2,64,128]{2,1,0:T(8,128)S(1)}, f32[2,64,128]{2,1,0:T(8,128)S(1)}, u32[]{:S(2)}, u32[]{:S(2)}) collective-permute-start(f32[2,64,128]{2,1,0:T(8,128)S(1)} %pad_maximum_fusion.own), channel_id=1, source_target_pairs={{0,64},{32,96},{64,0},{96,32},{1,65},{33,97},{65,1},{97,33},{2,66}... | collective-permute-start | bytes 196616 | tf_op jit(solution)/shard_map/ppermute | solution.py:596
  60.2 1.6 %collective-permute-start.5 = (f32[2,64,128]{2,1,0:T(8,128)S(1)}, f32[2,64,128]{2,1,0:T(8,128)S(1)}, u32[]{:S(2)}, u32[]{:S(2)}) collective-permute-start(f32[2,64,128]{2,1,0:T(8,128)S(1)} %pad_maximum_fusion.1), channel_id=1, source_target_pairs={{0,96},{32,64},{64,32},{96,0},{1,97},{33,65},{65,33},{97,1},{2,98}... | collective-permute-start | bytes 196616 | tf_op jit(solution)/shard_map/ppermute | solution.py:596
  61.7 0.0 collective-permute-start.3
  61.7 2.2 %collective-permute-done.4.by_grp = f32[2,64,128]{2,1,0:T(8,128)S(1)} collective-permute-done((f32[2,64,128]{2,1,0:T(8,128)S(1)}, f32[2,64,128]{2,1,0:T(8,128)S(1)}, u32[]{:S(2)}, u32[]{:S(2)}) %collective-permute-start.4) | collective-permute-done | bytes 65568 | tf_op jit(solution)/shard_map/ppermute | solution.py:596
  64.0 1.7 %collective-permute-done.5.by_both = f32[2,64,128]{2,1,0:T(8,128)S(1)} collective-permute-done((f32[2,64,128]{2,1,0:T(8,128)S(1)}, f32[2,64,128]{2,1,0:T(8,128)S(1)}, u32[]{:S(2)}, u32[]{:S(2)}) %collective-permute-start.5) | collective-permute-done | bytes 65568 | tf_op jit(solution)/shard_map/ppermute | solution.py:596
  65.6 0.4 collective-permute-done.3.by_row
  66.0 0.8 %assemble.1 = f32[4,2,64,128]{3,2,1,0:T(8,128)} custom-call(f32[2,64,128]{2,1,0:T(8,128)S(1)} %pad_maximum_fusion.own, f32[2,64,128]{2,1,0:T(8,128)S(1)} %collective-permute-done.3.by_row, f32[2,64,128]{2,1,0:T(8,128)S(1)} %collective-permute-done.4.by_grp, f32[2,64,128]{2,1,0:T(8,128)S(1)} %collective-permute-done.5.by_both), custom_call_target="tpu_custom_call" | custom-call | tf_op jit(solution)/shard_map/assemble/pallas_call | solution.py:537
  (5 shorter events, 0.0 us)
Async XLA Ops:
  0.0 1.8 %collective-permute-start = (f32[512,128]{1,0:T(8,128)}, f32[512,128]{1,0:T(8,128)S(1)}, u32[]{:S(2)}, u32[]{:S(2)}) collective-permute-start(f32[512,128]{1,0:T(8,128)} %bitcast.7), channel_id=1, source_target_pairs={{0,16},{16,0},{1,17},{17,1},{2,18},{18,2},{3,19},{19,3},{4,20},{20... | collective-permute-start | bytes 786440 | tf_op jit(solution)/shard_map/ppermute | solution.py:581
  0.0 2.1 %collective-permute-start.1 = (f32[512,128]{1,0:T(8,128)}, f32[512,128]{1,0:T(8,128)S(1)}, u32[]{:S(2)}, u32[]{:S(2)}) collective-permute-start(f32[512,128]{1,0:T(8,128)} %bitcast.9), channel_id=1, source_target_pairs={{0,16},{16,0},{1,17},{17,1},{2,18},{18,2},{3,19},{19,3},{4,20},{20... | collective-permute-start | bytes 786440 | tf_op jit(solution)/shard_map/ppermute | solution.py:582
  56.7 1.3 %collective-permute-start.2 = (f32[2,64,128]{2,1,0:T(8,128)S(1)}, f32[2,64,128]{2,1,0:T(8,128)S(1)}, u32[]{:S(2)}, u32[]{:S(2)}) collective-permute-start(f32[2,64,128]{2,1,0:T(8,128)S(1)} %slice.21), channel_id=1, source_target_pairs={{0,16},{16,0},{1,17},{17,1},{2,18},{18,2},{3,19},{19,3},{4,20},{20... | collective-permute-start | bytes 196616 | tf_op jit(solution)/shard_map/ppermute | solution.py:591
  58.1 5.9 %collective-permute-start.4 = (f32[2,64,128]{2,1,0:T(8,128)S(1)}, f32[2,64,128]{2,1,0:T(8,128)S(1)}, u32[]{:S(2)}, u32[]{:S(2)}) collective-permute-start(f32[2,64,128]{2,1,0:T(8,128)S(1)} %pad_maximum_fusion.own), channel_id=1, source_target_pairs={{0,64},{32,96},{64,0},{96,32},{1,65},{33,97},{65,1},{97,33},{2,66}... | collective-permute-start | bytes 196616 | tf_op jit(solution)/shard_map/ppermute | solution.py:596
  60.2 5.5 %collective-permute-start.5 = (f32[2,64,128]{2,1,0:T(8,128)S(1)}, f32[2,64,128]{2,1,0:T(8,128)S(1)}, u32[]{:S(2)}, u32[]{:S(2)}) collective-permute-start(f32[2,64,128]{2,1,0:T(8,128)S(1)} %pad_maximum_fusion.1), channel_id=1, source_target_pairs={{0,96},{32,64},{64,32},{96,0},{1,97},{33,65},{65,33},{97,1},{2,98}... | collective-permute-start | bytes 196616 | tf_op jit(solution)/shard_map/ppermute | solution.py:596
  61.7 4.3 %collective-permute-start.3 = (f32[2,64,128]{2,1,0:T(8,128)S(1)}, f32[2,64,128]{2,1,0:T(8,128)S(1)}, u32[]{:S(2)}, u32[]{:S(2)}) collective-permute-start(f32[2,64,128]{2,1,0:T(8,128)S(1)} %pad_maximum_fusion.1), channel_id=1, source_target_pairs={{0,32},{32,0},{64,96},{96,64},{1,33},{33,1},{65,97},{97,65},{2,34}... | collective-permute-start | bytes 196616 | tf_op jit(solution)/shard_map/ppermute | solution.py:596

commit v5 on v4

--- a/solution.py
+++ b/solution.py
@@ -375,7 +375,7 @@
         send(1, c)
 
 
-def rows_inverse(received, tables, columns, out, z_full, z_half):
+def rows_inverse(received, tables, columns, keep, send, z_full, z_half):
     row = lax.axis_index("ylo") * 2 + lax.axis_index("core")
     mine = lax.axis_index("grp") * 4 + row
     even = ((lax.broadcasted_iota(jnp.int32, (16, 128), 1) - 16 * mine) & 16) == 0
@@ -396,6 +396,7 @@
         parts = [chunk(56 + 4 * s + u) for u in range(4)]
         z_half[s] = table_times(tables[1280:1536, 128 * s : 128 * s + 128], jnp.concatenate([p[k] for p in parts for k in range(2)], axis=0))
     lane = lax.broadcasted_iota(jnp.int32, (8, 128), 1) - 16 * mine
+    on_even = (row & 1) == 0
     low64, low32, low16 = (lane & 64) == 0, (lane & 32) == 0, (lane & 16) == 0
 
     def fold(one, two, low, shift):
@@ -404,14 +405,18 @@
 
     for slab in range(8):
         x = [fields_of(slab + 8 * h, z_full, z_half, columns) for h in range(2)]
+        pieces = []
         for dest in range(4):
             u = []
             for m in range(4 * dest, 4 * dest + 4):
                 one, two = x[0][m], x[1][m]
                 u.append(jnp.where(low64, one, two) * pltpu.roll(jnp.where(low64, two, one), 64, 1))
             packed = fold(fold(u[0], u[2], low32, 32), fold(u[1], u[3], low32, 32), low16, 16)
-            slot = dest ^ row
-            out[((slot & 1) << 1) | (slot >> 1), pl.ds(slab * 8, 8), :] = packed
+            pieces.append(packed)
+        for ylo in range(2):
+            even_core, odd_core = pieces[2 * ylo], pieces[2 * ylo + 1]
+            keep[ylo ^ (row >> 1), pl.ds(slab * 8, 8), :] = jnp.where(on_even, even_core, odd_core)
+            send[ylo ^ (row >> 1), pl.ds(slab * 8, 8), :] = jnp.where(on_even, odd_core, even_core)
 
 
 def fields_of(slab, z_full, z_half, columns):
@@ -524,9 +529,9 @@
 def call_rows_inverse(filtered, tables, columns):
     return pl.pallas_call(
         rows_inverse,
-        out_shape=shape(4, 64, 128),
+        out_shape=(shape(2, 64, 128), shape(2, 64, 128)),
         in_specs=in_vmem(3),
-        out_specs=in_vmem(1)[0],
+        out_specs=tuple(in_vmem(2)),
         scratch_shapes=[pltpu.VMEM((7, 256, 128), F32), pltpu.VMEM((2, 128, 128), F32)],
         compiler_params=params(),
         name="rows_inverse",
@@ -587,10 +592,10 @@
     spectra = lax.all_to_all(spectra.reshape(64, 32, 128), FIRST, split_axis=0, concat_axis=0, tiled=True)
     filtered = call_cols_filter(spectra, straight, mirrored, tables, columns)
     filtered = lax.all_to_all(filtered, SECOND, split_axis=0, concat_axis=0, tiled=True)
-    products = call_rows_inverse(filtered, tables, columns)
-    got = lax.ppermute(products[2:4], "core", swap_cores)
-    near = jnp.stack([products[0], got[0]])
-    far = jnp.stack([products[1], got[1]])
+    keep, send = call_rows_inverse(filtered, tables, columns)
+    got = lax.ppermute(send, "core", swap_cores)
+    near = jnp.stack([keep[0], got[0]])
+    far = jnp.stack([keep[1], got[1]])
 
     def exchange(value, step):
         return lax.ppermute(value, ("grp", "ylo"), [(i, i ^ step) for i in range(4)])

time: 67 us -> 67 us (level)
  no operation moved by 1% of the time
where the time goes in v5:
time: 67 us; the launch traced here: 66.8 us
  blocking collectives  51.2 us (76%)
  waiting for transfers between devices  5.77 us (9%)
  Pallas kernels  5.58 us (8%)
  starting transfers between devices  4.22 us (6%)
    all_to_all x1, blocking collectives, on_device(): lax.all_to_all(spectra.reshape(64, 32, 128), FIRST, split_axis=0, concat_...  26.5 us
    all_to_all x1, blocking collectives, on_device(): lax.all_to_all(filtered, SECOND, split_axis=0, concat_axis=0, tiled=True)  24.6 us
    ppermute x3, waiting for transfers between devices, exchange(): lax.ppermute(value, ('grp', 'ylo'), [(i, i ^ step) for i in range(4)])  4.26 us
    ppermute x3, starting transfers between devices, exchange(): lax.ppermute(value, ('grp', 'ylo'), [(i, i ^ step) for i in range(4)])  3.63 us
    pallas_call x1, Pallas kernels, call_cols_filter(): pl.pallas_call(cols_filter, out_shape=shape(128, 16, 128), in_specs=in_vm...  1.38 us
  transfers between devices with their start and end apart: 6, of which 5 were waited for; matrix products, arithmetic and copies ran while one was open for 0% of the time, Pallas kernels for 2%

profile of v5, /device:TPU:0, one launch (start us, length us, event | category | flops | bytes accessed | tf_op | source)
XLA Modules:
  0.0 66.8 jit_solution(5523751054546565418)
XLA Ops:
  0.0 0.0 collective-permute-start
  0.0 0.5 collective-permute-start.1
  0.5 1.3 %front.1 = (f32[512,128]{1,0:T(8,128)S(1)}, bf16[1536,256]{1,0:T(8,128)(2,1)S(1)}, f32[160,128]{1,0:T(8,128)S(1)}, f32[2,4,16,128]{3,2,1,0:T(8,128)S(1)}, f32[2,4,8,128]{3,2,1,0:T(8,128)S(1)}) custom-call(f32[512,128]{1,0:T(8,128)} %bitcast.8, f32[512,128]{1,0:T(8,128)} %bitcast.10, bf16[1536,256]{1,0:T(8,128)(2,1)} %constant.4.clone.tables, ...), custom_call_target="tpu_custom_call" | custom-call | tf_op jit(solution)/shard_map/front/pallas_call | solution.py:558
  1.8 0.0 collective-permute-done.got_members
  1.8 0.3 collective-permute-done.1.got_control
  2.1 0.8 %rows_forward.1 = f32[2048,128]{1,0:T(8,128)S(1)} custom-call(f32[512,128]{1,0:T(8,128)S(1)} %get-tuple-element.12.own, f32[512,128]{1,0:T(8,128)S(1)} %collective-permute-done.got_members, f32[512,128]{1,0:T(8,128)S(1)} %collective-permute-done.1.got_control, bf16[1536,256]{1,0:T(8,128)(2,1)S(1)} %get-tuple-element.13.tables, ...), custom_call_target="tpu_custom_call" | custom-call | tf_op jit(solution)/shard_map/rows_forward/pallas_call | solution.py:502
  3.0 26.5 %all_to_all.10.received = f32[64,32,128]{2,1,0:T(8,128)S(1)} all-to-all(f32[64,32,128]{2,1,0:T(8,128)S(1)} %bitcast.6), channel_id=1, replica_groups=mesh['grp'=2,'ylo'=2,'core'=2,'x1'=2,'x0'=2,'z1'=2,'z0'=2] {'x1','x0','c..., dimensions={0} | all-to-all | bytes 2097152 | tf_op jit(solution)/shard_map/all_to_all | solution.py:592
  29.5 1.4 %cols_filter.1 = f32[128,16,128]{2,1,0:T(8,128)S(1)} custom-call(f32[64,32,128]{2,1,0:T(8,128)S(1)} %all_to_all.10.received, f32[2,4,16,128]{3,2,1,0:T(8,128)S(1)} %get-tuple-element.15.straight, f32[2,4,8,128]{3,2,1,0:T(8,128)S(1)} %get-tuple-element.16.mirrored, bf16[1536,256]{1,0:T(8,128)(2,1)S(1)} %get-tuple-element.13.tables, ...), custom_call_target="tpu_custom_call" | custom-call | tf_op jit(solution)/shard_map/cols_filter/pallas_call | solution.py:514
  30.9 24.6 %all_to_all.11.received = f32[128,16,128]{2,1,0:T(8,128)S(1)} all-to-all(f32[128,16,128]{2,1,0:T(8,128)S(1)} %cols_filter.1), channel_id=1, replica_groups=mesh['grp'=2,'ylo'=2,'core'=2,'x1'=2,'x0'=2,'z1'=2,'z0'=2] {'core','z1',..., dimensions={0} | all-to-all | bytes 2097152 | tf_op jit(solution)/shard_map/all_to_all | solution.py:594
  55.5 1.2 %rows_inverse.1 = (f32[2,64,128]{2,1,0:T(8,128)S(1)}, f32[2,64,128]{2,1,0:T(8,128)S(1)}) custom-call(f32[128,16,128]{2,1,0:T(8,128)S(1)} %all_to_all.11.received, bf16[1536,256]{1,0:T(8,128)(2,1)S(1)} %get-tuple-element.13.tables, f32[160,128]{1,0:T(8,128)S(1)} %get-tuple-element.14.columns), custom_call_target="tpu_custom_call" | custom-call | tf_op jit(solution)/shard_map/rows_inverse/pallas_call | solution.py:530
  56.7 0.1 collective-permute-start.2
  56.8 1.2 %collective-permute-done.2 = f32[2,64,128]{2,1,0:T(8,128)S(1)} collective-permute-done((f32[2,64,128]{2,1,0:T(8,128)S(1)}, f32[2,64,128]{2,1,0:T(8,128)S(1)}, u32[]{:S(2)}, u32[]{:S(2)}) %collective-permute-start.2) | collective-permute-done | bytes 65568 | tf_op jit(solution)/shard_map/ppermute | solution.py:596
  58.1 2.1 %collective-permute-start.4 = (f32[2,64,128]{2,1,0:T(8,128)S(1)}, f32[2,64,128]{2,1,0:T(8,128)S(1)}, u32[]{:S(2)}, u32[]{:S(2)}) collective-permute-start(f32[2,64,128]{2,1,0:T(8,128)S(1)} %pad_maximum_fusion.own), channel_id=1, source_target_pairs={{0,64},{32,96},{64,0},{96,32},{1,65},{33,97},{65,1},{97,33},{2,66}... | collective-permute-start | bytes 196616 | tf_op jit(solution)/shard_map/ppermute | solution.py:601
  60.2 1.6 %collective-permute-start.5 = (f32[2,64,128]{2,1,0:T(8,128)S(1)}, f32[2,64,128]{2,1,0:T(8,128)S(1)}, u32[]{:S(2)}, u32[]{:S(2)}) collective-permute-start(f32[2,64,128]{2,1,0:T(8,128)S(1)} %pad_maximum_fusion.1), channel_id=1, source_target_pairs={{0,96},{32,64},{64,32},{96,0},{1,97},{33,65},{65,33},{97,1},{2,98}... | collective-permute-start | bytes 196616 | tf_op jit(solution)/shard_map/ppermute | solution.py:601
  61.7 0.0 collective-permute-start.3
  61.7 2.2 %collective-permute-done.4.by_grp = f32[2,64,128]{2,1,0:T(8,128)S(1)} collective-permute-done((f32[2,64,128]{2,1,0:T(8,128)S(1)}, f32[2,64,128]{2,1,0:T(8,128)S(1)}, u32[]{:S(2)}, u32[]{:S(2)}) %collective-permute-start.4) | collective-permute-done | bytes 65568 | tf_op jit(solution)/shard_map/ppermute | solution.py:601
  63.9 1.7 %collective-permute-done.5.by_both = f32[2,64,128]{2,1,0:T(8,128)S(1)} collective-permute-done((f32[2,64,128]{2,1,0:T(8,128)S(1)}, f32[2,64,128]{2,1,0:T(8,128)S(1)}, u32[]{:S(2)}, u32[]{:S(2)}) %collective-permute-start.5) | collective-permute-done | bytes 65568 | tf_op jit(solution)/shard_map/ppermute | solution.py:601
  65.6 0.4 collective-permute-done.3.by_row
  66.0 0.8 %assemble.1 = f32[4,2,64,128]{3,2,1,0:T(8,128)} custom-call(f32[2,64,128]{2,1,0:T(8,128)S(1)} %pad_maximum_fusion.own, f32[2,64,128]{2,1,0:T(8,128)S(1)} %collective-permute-done.3.by_row, f32[2,64,128]{2,1,0:T(8,128)S(1)} %collective-permute-done.4.by_grp, f32[2,64,128]{2,1,0:T(8,128)S(1)} %collective-permute-done.5.by_both), custom_call_target="tpu_custom_call" | custom-call | tf_op jit(solution)/shard_map/assemble/pallas_call | solution.py:542
  (4 shorter events, 0.0 us)
Async XLA Ops:
  0.0 1.8 %collective-permute-start = (f32[512,128]{1,0:T(8,128)}, f32[512,128]{1,0:T(8,128)S(1)}, u32[]{:S(2)}, u32[]{:S(2)}) collective-permute-start(f32[512,128]{1,0:T(8,128)} %bitcast.7), channel_id=1, source_target_pairs={{0,16},{16,0},{1,17},{17,1},{2,18},{18,2},{3,19},{19,3},{4,20},{20... | collective-permute-start | bytes 786440 | tf_op jit(solution)/shard_map/ppermute | solution.py:586
  0.0 2.1 %collective-permute-start.1 = (f32[512,128]{1,0:T(8,128)}, f32[512,128]{1,0:T(8,128)S(1)}, u32[]{:S(2)}, u32[]{:S(2)}) collective-permute-start(f32[512,128]{1,0:T(8,128)} %bitcast.9), channel_id=1, source_target_pairs={{0,16},{16,0},{1,17},{17,1},{2,18},{18,2},{3,19},{19,3},{4,20},{20... | collective-permute-start | bytes 786440 | tf_op jit(solution)/shard_map/ppermute | solution.py:587
  56.7 1.3 %collective-permute-start.2 = (f32[2,64,128]{2,1,0:T(8,128)S(1)}, f32[2,64,128]{2,1,0:T(8,128)S(1)}, u32[]{:S(2)}, u32[]{:S(2)}) collective-permute-start(f32[2,64,128]{2,1,0:T(8,128)S(1)} %get-tuple-element.18), channel_id=1, source_target_pairs={{0,16},{16,0},{1,17},{17,1},{2,18},{18,2},{3,19},{19,3},{4,20},{20... | collective-permute-start | bytes 196616 | tf_op jit(solution)/shard_map/ppermute | solution.py:596
  58.1 5.9 %collective-permute-start.4 = (f32[2,64,128]{2,1,0:T(8,128)S(1)}, f32[2,64,128]{2,1,0:T(8,128)S(1)}, u32[]{:S(2)}, u32[]{:S(2)}) collective-permute-start(f32[2,64,128]{2,1,0:T(8,128)S(1)} %pad_maximum_fusion.own), channel_id=1, source_target_pairs={{0,64},{32,96},{64,0},{96,32},{1,65},{33,97},{65,1},{97,33},{2,66}... | collective-permute-start | bytes 196616 | tf_op jit(solution)/shard_map/ppermute | solution.py:601
  60.2 5.5 %collective-permute-start.5 = (f32[2,64,128]{2,1,0:T(8,128)S(1)}, f32[2,64,128]{2,1,0:T(8,128)S(1)}, u32[]{:S(2)}, u32[]{:S(2)}) collective-permute-start(f32[2,64,128]{2,1,0:T(8,128)S(1)} %pad_maximum_fusion.1), channel_id=1, source_target_pairs={{0,96},{32,64},{64,32},{96,0},{1,97},{33,65},{65,33},{97,1},{2,98}... | collective-permute-start | bytes 196616 | tf_op jit(solution)/shard_map/ppermute | solution.py:601
  61.7 4.3 %collective-permute-start.3 = (f32[2,64,128]{2,1,0:T(8,128)S(1)}, f32[2,64,128]{2,1,0:T(8,128)S(1)}, u32[]{:S(2)}, u32[]{:S(2)}) collective-permute-start(f32[2,64,128]{2,1,0:T(8,128)S(1)} %pad_maximum_fusion.1), channel_id=1, source_target_pairs={{0,32},{32,0},{64,96},{96,64},{1,33},{33,1},{65,97},{97,65},{2,34}... | collective-permute-start | bytes 196616 | tf_op jit(solution)/shard_map/ppermute | solution.py:601

commit v6 on v4

--- a/solution.py
+++ b/solution.py
@@ -60,7 +60,7 @@
 
 
 AXES = ("grp", "ylo", "core", "x1", "x0", "z1", "z0")
-FIRST = ("x1", "x0", "core", "z1", "ylo", "z0")
+FIRST = ("x0", "x1", "core", "z1", "ylo", "z0")
 SECOND = ("core", "z1", "z0", "x1", "x0", "grp", "ylo")
 
 

time: 67 us -> 67 us (level)
  no operation moved by 1% of the time
where the time goes in v6:
time: 67 us; the launch traced here: 66.9 us
  blocking collectives  51.2 us (76%)
  waiting for transfers between devices  5.77 us (9%)
  Pallas kernels  5.59 us (8%)
  starting transfers between devices  4.21 us (6%)
    all_to_all x1, blocking collectives, on_device(): lax.all_to_all(spectra.reshape(64, 32, 128), FIRST, split_axis=0, concat_...  27.1 us
    all_to_all x1, blocking collectives, on_device(): lax.all_to_all(filtered, SECOND, split_axis=0, concat_axis=0, tiled=True)  24.1 us
    ppermute x3, waiting for transfers between devices, exchange(): lax.ppermute(value, ('grp', 'ylo'), [(i, i ^ step) for i in range(4)])  4.26 us
    ppermute x3, starting transfers between devices, exchange(): lax.ppermute(value, ('grp', 'ylo'), [(i, i ^ step) for i in range(4)])  3.62 us
    pallas_call x1, Pallas kernels, call_cols_filter(): pl.pallas_call(cols_filter, out_shape=shape(128, 16, 128), in_specs=in_vm...  1.38 us
  transfers between devices with their start and end apart: 6, of which 5 were waited for; matrix products, arithmetic and copies ran while one was open for 0% of the time, Pallas kernels for 2%

profile of v6, /device:TPU:0, one launch (start us, length us, event | category | flops | bytes accessed | tf_op | source)
XLA Modules:
  0.0 66.9 jit_solution(9368208931688796658)
XLA Ops:
  0.0 0.0 collective-permute-start
  0.0 0.5 collective-permute-start.1
  0.5 1.3 %front.1 = (f32[512,128]{1,0:T(8,128)S(1)}, bf16[1536,256]{1,0:T(8,128)(2,1)S(1)}, f32[160,128]{1,0:T(8,128)S(1)}, f32[2,4,16,128]{3,2,1,0:T(8,128)S(1)}, f32[2,4,8,128]{3,2,1,0:T(8,128)S(1)}) custom-call(f32[512,128]{1,0:T(8,128)} %bitcast.8, f32[512,128]{1,0:T(8,128)} %bitcast.10, bf16[1536,256]{1,0:T(8,128)(2,1)} %constant.4.clone.tables, ...), custom_call_target="tpu_custom_call" | custom-call | tf_op jit(solution)/shard_map/front/pallas_call | solution.py:553
  1.8 0.0 collective-permute-done.got_members
  1.8 0.3 collective-permute-done.1.got_control
  2.1 0.8 %rows_forward.1 = f32[2048,128]{1,0:T(8,128)S(1)} custom-call(f32[512,128]{1,0:T(8,128)S(1)} %get-tuple-element.10.own, f32[512,128]{1,0:T(8,128)S(1)} %collective-permute-done.got_members, f32[512,128]{1,0:T(8,128)S(1)} %collective-permute-done.1.got_control, bf16[1536,256]{1,0:T(8,128)(2,1)S(1)} %get-tuple-element.11.tables, ...), custom_call_target="tpu_custom_call" | custom-call | tf_op jit(solution)/shard_map/rows_forward/pallas_call | solution.py:497
  3.0 27.1 %all_to_all.10.received = f32[64,32,128]{2,1,0:T(8,128)S(1)} all-to-all(f32[64,32,128]{2,1,0:T(8,128)S(1)} %bitcast.6), channel_id=1, replica_groups=mesh['grp'=2,'ylo'=2,'core'=2,'x1'=2,'x0'=2,'z1'=2,'z0'=2] {'x0','x1','c..., dimensions={0} | all-to-all | bytes 2097152 | tf_op jit(solution)/shard_map/all_to_all | solution.py:587
  30.0 1.4 %cols_filter.1 = f32[128,16,128]{2,1,0:T(8,128)S(1)} custom-call(f32[64,32,128]{2,1,0:T(8,128)S(1)} %all_to_all.10.received, f32[2,4,16,128]{3,2,1,0:T(8,128)S(1)} %get-tuple-element.13.straight, f32[2,4,8,128]{3,2,1,0:T(8,128)S(1)} %get-tuple-element.14.mirrored, bf16[1536,256]{1,0:T(8,128)(2,1)S(1)} %get-tuple-element.11.tables, ...), custom_call_target="tpu_custom_call" | custom-call | tf_op jit(solution)/shard_map/cols_filter/pallas_call | solution.py:509
  31.4 24.1 %all_to_all.11.received = f32[128,16,128]{2,1,0:T(8,128)S(1)} all-to-all(f32[128,16,128]{2,1,0:T(8,128)S(1)} %cols_filter.1), channel_id=1, replica_groups=mesh['grp'=2,'ylo'=2,'core'=2,'x1'=2,'x0'=2,'z1'=2,'z0'=2] {'core','z1',..., dimensions={0} | all-to-all | bytes 2097152 | tf_op jit(solution)/shard_map/all_to_all | solution.py:589
  55.5 1.2 %rows_inverse.1 = f32[4,64,128]{2,1,0:T(8,128)S(1)} custom-call(f32[128,16,128]{2,1,0:T(8,128)S(1)} %all_to_all.11.received, bf16[1536,256]{1,0:T(8,128)(2,1)S(1)} %get-tuple-element.11.tables, f32[160,128]{1,0:T(8,128)S(1)} %get-tuple-element.12.columns), custom_call_target="tpu_custom_call" | custom-call | tf_op jit(solution)/shard_map/rows_inverse/pallas_call | solution.py:525
  56.8 0.1 collective-permute-start.2
  56.9 1.2 %collective-permute-done.2 = f32[2,64,128]{2,1,0:T(8,128)S(1)} collective-permute-done((f32[2,64,128]{2,1,0:T(8,128)S(1)}, f32[2,64,128]{2,1,0:T(8,128)S(1)}, u32[]{:S(2)}, u32[]{:S(2)}) %collective-permute-start.2) | collective-permute-done | bytes 65568 | tf_op jit(solution)/shard_map/ppermute | solution.py:591
  58.1 2.1 %collective-permute-start.4 = (f32[2,64,128]{2,1,0:T(8,128)S(1)}, f32[2,64,128]{2,1,0:T(8,128)S(1)}, u32[]{:S(2)}, u32[]{:S(2)}) collective-permute-start(f32[2,64,128]{2,1,0:T(8,128)S(1)} %pad_maximum_fusion.own), channel_id=1, source_target_pairs={{0,64},{32,96},{64,0},{96,32},{1,65},{33,97},{65,1},{97,33},{2,66}... | collective-permute-start | bytes 196616 | tf_op jit(solution)/shard_map/ppermute | solution.py:596
  60.2 1.6 %collective-permute-start.5 = (f32[2,64,128]{2,1,0:T(8,128)S(1)}, f32[2,64,128]{2,1,0:T(8,128)S(1)}, u32[]{:S(2)}, u32[]{:S(2)}) collective-permute-start(f32[2,64,128]{2,1,0:T(8,128)S(1)} %pad_maximum_fusion.1), channel_id=1, source_target_pairs={{0,96},{32,64},{64,32},{96,0},{1,97},{33,65},{65,33},{97,1},{2,98}... | collective-permute-start | bytes 196616 | tf_op jit(solution)/shard_map/ppermute | solution.py:596
  61.8 0.0 collective-permute-start.3
  61.8 2.2 %collective-permute-done.4.by_grp = f32[2,64,128]{2,1,0:T(8,128)S(1)} collective-permute-done((f32[2,64,128]{2,1,0:T(8,128)S(1)}, f32[2,64,128]{2,1,0:T(8,128)S(1)}, u32[]{:S(2)}, u32[]{:S(2)}) %collective-permute-start.4) | collective-permute-done | bytes 65568 | tf_op jit(solution)/shard_map/ppermute | solution.py:596
  64.0 1.7 %collective-permute-done.5.by_both = f32[2,64,128]{2,1,0:T(8,128)S(1)} collective-permute-done((f32[2,64,128]{2,1,0:T(8,128)S(1)}, f32[2,64,128]{2,1,0:T(8,128)S(1)}, u32[]{:S(2)}, u32[]{:S(2)}) %collective-permute-start.5) | collective-permute-done | bytes 65568 | tf_op jit(solution)/shard_map/ppermute | solution.py:596
  65.7 0.3 collective-permute-done.3.by_row
  66.0 0.8 %assemble.1 = f32[4,2,64,128]{3,2,1,0:T(8,128)} custom-call(f32[2,64,128]{2,1,0:T(8,128)S(1)} %pad_maximum_fusion.own, f32[2,64,128]{2,1,0:T(8,128)S(1)} %collective-permute-done.3.by_row, f32[2,64,128]{2,1,0:T(8,128)S(1)} %collective-permute-done.4.by_grp, f32[2,64,128]{2,1,0:T(8,128)S(1)} %collective-permute-done.5.by_both), custom_call_target="tpu_custom_call" | custom-call | tf_op jit(solution)/shard_map/assemble/pallas_call | solution.py:537
  (5 shorter events, 0.0 us)
Async XLA Ops:
  0.0 1.8 %collective-permute-start = (f32[512,128]{1,0:T(8,128)}, f32[512,128]{1,0:T(8,128)S(1)}, u32[]{:S(2)}, u32[]{:S(2)}) collective-permute-start(f32[512,128]{1,0:T(8,128)} %bitcast.7), channel_id=1, source_target_pairs={{0,16},{16,0},{1,17},{17,1},{2,18},{18,2},{3,19},{19,3},{4,20},{20... | collective-permute-start | bytes 786440 | tf_op jit(solution)/shard_map/ppermute | solution.py:581
  0.0 2.1 %collective-permute-start.1 = (f32[512,128]{1,0:T(8,128)}, f32[512,128]{1,0:T(8,128)S(1)}, u32[]{:S(2)}, u32[]{:S(2)}) collective-permute-start(f32[512,128]{1,0:T(8,128)} %bitcast.9), channel_id=1, source_target_pairs={{0,16},{16,0},{1,17},{17,1},{2,18},{18,2},{3,19},{19,3},{4,20},{20... | collective-permute-start | bytes 786440 | tf_op jit(solution)/shard_map/ppermute | solution.py:582
  56.8 1.3 %collective-permute-start.2 = (f32[2,64,128]{2,1,0:T(8,128)S(1)}, f32[2,64,128]{2,1,0:T(8,128)S(1)}, u32[]{:S(2)}, u32[]{:S(2)}) collective-permute-start(f32[2,64,128]{2,1,0:T(8,128)S(1)} %slice.21), channel_id=1, source_target_pairs={{0,16},{16,0},{1,17},{17,1},{2,18},{18,2},{3,19},{19,3},{4,20},{20... | collective-permute-start | bytes 196616 | tf_op jit(solution)/shard_map/ppermute | solution.py:591
  58.1 5.9 %collective-permute-start.4 = (f32[2,64,128]{2,1,0:T(8,128)S(1)}, f32[2,64,128]{2,1,0:T(8,128)S(1)}, u32[]{:S(2)}, u32[]{:S(2)}) collective-permute-start(f32[2,64,128]{2,1,0:T(8,128)S(1)} %pad_maximum_fusion.own), channel_id=1, source_target_pairs={{0,64},{32,96},{64,0},{96,32},{1,65},{33,97},{65,1},{97,33},{2,66}... | collective-permute-start | bytes 196616 | tf_op jit(solution)/shard_map/ppermute | solution.py:596
  60.2 5.5 %collective-permute-start.5 = (f32[2,64,128]{2,1,0:T(8,128)S(1)}, f32[2,64,128]{2,1,0:T(8,128)S(1)}, u32[]{:S(2)}, u32[]{:S(2)}) collective-permute-start(f32[2,64,128]{2,1,0:T(8,128)S(1)} %pad_maximum_fusion.1), channel_id=1, source_target_pairs={{0,96},{32,64},{64,32},{96,0},{1,97},{33,65},{65,33},{97,1},{2,98}... | collective-permute-start | bytes 196616 | tf_op jit(solution)/shard_map/ppermute | solution.py:596
  61.8 4.3 %collective-permute-start.3 = (f32[2,64,128]{2,1,0:T(8,128)S(1)}, f32[2,64,128]{2,1,0:T(8,128)S(1)}, u32[]{:S(2)}, u32[]{:S(2)}) collective-permute-start(f32[2,64,128]{2,1,0:T(8,128)S(1)} %pad_maximum_fusion.1), channel_id=1, source_target_pairs={{0,32},{32,0},{64,96},{96,64},{1,33},{33,1},{65,97},{97,65},{2,34}... | collective-permute-start | bytes 196616 | tf_op jit(solution)/shard_map/ppermute | solution.py:596

commit v7 on v4

--- a/solution.py
+++ b/solution.py
@@ -450,13 +450,13 @@
         pieces[pl.ds(2 * k, 2)] = ref[...]
     lane = lax.broadcasted_iota(jnp.int32, (8, 128), 1)
     copies = []
-    for part in range(2):
-        for slab in range(4 * part, 4 * part + 4):
+    for part in range(4):
+        for slab in range(2 * part, 2 * part + 2):
             rows = pl.ds(slab * 8, 8)
             for i, moved in enumerate(diagonals([pieces[q ^ mine, rows, :] for q in range(8)], lane)):
                 e = -i % 8
                 whole[e & 3, e >> 2, rows, :] = pltpu.roll(moved, 16 * i, 1) if i else moved
-        rows = pl.ds(32 * part, 32)
+        rows = pl.ds(16 * part, 16)
         copy = pltpu.make_async_copy(whole.at[:, :, rows, :], out.at[:, :, rows, :], sems.at[part])
         copy.start()
         copies.append(copy)
@@ -542,7 +542,7 @@
         scratch_shapes=[
             pltpu.VMEM((8, 64, 128), F32),
             pltpu.VMEM((4, 2, 64, 128), F32),
-            pltpu.SemaphoreType.DMA((2,)),
+            pltpu.SemaphoreType.DMA((4,)),
         ],
         compiler_params=params(),
         name="assemble",

time: 67 us -> 67 us (level)
  no operation moved by 1% of the time
where the time goes in v7:
time: 67 us; the launch traced here: 66.8 us
  blocking collectives  51.2 us (76%)
  waiting for transfers between devices  5.77 us (9%)
  Pallas kernels  5.58 us (8%)
  starting transfers between devices  4.22 us (6%)
    all_to_all x1, blocking collectives, on_device(): lax.all_to_all(spectra.reshape(64, 32, 128), FIRST, split_axis=0, concat_...  26.5 us
    all_to_all x1, blocking collectives, on_device(): lax.all_to_all(filtered, SECOND, split_axis=0, concat_axis=0, tiled=True)  24.6 us
    ppermute x3, waiting for transfers between devices, exchange(): lax.ppermute(value, ('grp', 'ylo'), [(i, i ^ step) for i in range(4)])  4.26 us
    ppermute x3, starting transfers between devices, exchange(): lax.ppermute(value, ('grp', 'ylo'), [(i, i ^ step) for i in range(4)])  3.63 us
    pallas_call x1, Pallas kernels, call_cols_filter(): pl.pallas_call(cols_filter, out_shape=shape(128, 16, 128), in_specs=in_vm...  1.38 us
  transfers between devices with their start and end apart: 6, of which 5 were waited for; matrix products, arithmetic and copies ran while one was open for 0% of the time, Pallas kernels for 2%

profile of v7, /device:TPU:0, one launch (start us, length us, event | category | flops | bytes accessed | tf_op | source)
XLA Modules:
  0.0 66.8 jit_solution(9447914689957476902)
XLA Ops:
  0.0 0.0 collective-permute-start
  0.0 0.5 collective-permute-start.1
  0.5 1.3 %front.1 = (f32[512,128]{1,0:T(8,128)S(1)}, bf16[1536,256]{1,0:T(8,128)(2,1)S(1)}, f32[160,128]{1,0:T(8,128)S(1)}, f32[2,4,16,128]{3,2,1,0:T(8,128)S(1)}, f32[2,4,8,128]{3,2,1,0:T(8,128)S(1)}) custom-call(f32[512,128]{1,0:T(8,128)} %bitcast.8, f32[512,128]{1,0:T(8,128)} %bitcast.10, bf16[1536,256]{1,0:T(8,128)(2,1)} %constant.4.clone.tables, ...), custom_call_target="tpu_custom_call" | custom-call | tf_op jit(solution)/shard_map/front/pallas_call | solution.py:553
  1.8 0.0 collective-permute-done.got_members
  1.8 0.3 collective-permute-done.1.got_control
  2.1 0.8 %rows_forward.1 = f32[2048,128]{1,0:T(8,128)S(1)} custom-call(f32[512,128]{1,0:T(8,128)S(1)} %get-tuple-element.10.own, f32[512,128]{1,0:T(8,128)S(1)} %collective-permute-done.got_members, f32[512,128]{1,0:T(8,128)S(1)} %collective-permute-done.1.got_control, bf16[1536,256]{1,0:T(8,128)(2,1)S(1)} %get-tuple-element.11.tables, ...), custom_call_target="tpu_custom_call" | custom-call | tf_op jit(solution)/shard_map/rows_forward/pallas_call | solution.py:497
  3.0 26.5 %all_to_all.10.received = f32[64,32,128]{2,1,0:T(8,128)S(1)} all-to-all(f32[64,32,128]{2,1,0:T(8,128)S(1)} %bitcast.6), channel_id=1, replica_groups=mesh['grp'=2,'ylo'=2,'core'=2,'x1'=2,'x0'=2,'z1'=2,'z0'=2] {'x1','x0','c..., dimensions={0} | all-to-all | bytes 2097152 | tf_op jit(solution)/shard_map/all_to_all | solution.py:587
  29.5 1.4 %cols_filter.1 = f32[128,16,128]{2,1,0:T(8,128)S(1)} custom-call(f32[64,32,128]{2,1,0:T(8,128)S(1)} %all_to_all.10.received, f32[2,4,16,128]{3,2,1,0:T(8,128)S(1)} %get-tuple-element.13.straight, f32[2,4,8,128]{3,2,1,0:T(8,128)S(1)} %get-tuple-element.14.mirrored, bf16[1536,256]{1,0:T(8,128)(2,1)S(1)} %get-tuple-element.11.tables, ...), custom_call_target="tpu_custom_call" | custom-call | tf_op jit(solution)/shard_map/cols_filter/pallas_call | solution.py:509
  30.9 24.6 %all_to_all.11.received = f32[128,16,128]{2,1,0:T(8,128)S(1)} all-to-all(f32[128,16,128]{2,1,0:T(8,128)S(1)} %cols_filter.1), channel_id=1, replica_groups=mesh['grp'=2,'ylo'=2,'core'=2,'x1'=2,'x0'=2,'z1'=2,'z0'=2] {'core','z1',..., dimensions={0} | all-to-all | bytes 2097152 | tf_op jit(solution)/shard_map/all_to_all | solution.py:589
  55.5 1.2 %rows_inverse.1 = f32[4,64,128]{2,1,0:T(8,128)S(1)} custom-call(f32[128,16,128]{2,1,0:T(8,128)S(1)} %all_to_all.11.received, bf16[1536,256]{1,0:T(8,128)(2,1)S(1)} %get-tuple-element.11.tables, f32[160,128]{1,0:T(8,128)S(1)} %get-tuple-element.12.columns), custom_call_target="tpu_custom_call" | custom-call | tf_op jit(solution)/shard_map/rows_inverse/pallas_call | solution.py:525
  56.7 0.1 collective-permute-start.2
  56.9 1.2 %collective-permute-done.2 = f32[2,64,128]{2,1,0:T(8,128)S(1)} collective-permute-done((f32[2,64,128]{2,1,0:T(8,128)S(1)}, f32[2,64,128]{2,1,0:T(8,128)S(1)}, u32[]{:S(2)}, u32[]{:S(2)}) %collective-permute-start.2) | collective-permute-done | bytes 65568 | tf_op jit(solution)/shard_map/ppermute | solution.py:591
  58.1 2.1 %collective-permute-start.4 = (f32[2,64,128]{2,1,0:T(8,128)S(1)}, f32[2,64,128]{2,1,0:T(8,128)S(1)}, u32[]{:S(2)}, u32[]{:S(2)}) collective-permute-start(f32[2,64,128]{2,1,0:T(8,128)S(1)} %pad_maximum_fusion.own), channel_id=1, source_target_pairs={{0,64},{32,96},{64,0},{96,32},{1,65},{33,97},{65,1},{97,33},{2,66}... | collective-permute-start | bytes 196616 | tf_op jit(solution)/shard_map/ppermute | solution.py:596
  60.2 1.6 %collective-permute-start.5 = (f32[2,64,128]{2,1,0:T(8,128)S(1)}, f32[2,64,128]{2,1,0:T(8,128)S(1)}, u32[]{:S(2)}, u32[]{:S(2)}) collective-permute-start(f32[2,64,128]{2,1,0:T(8,128)S(1)} %pad_maximum_fusion.1), channel_id=1, source_target_pairs={{0,96},{32,64},{64,32},{96,0},{1,97},{33,65},{65,33},{97,1},{2,98}... | collective-permute-start | bytes 196616 | tf_op jit(solution)/shard_map/ppermute | solution.py:596
  61.7 0.0 collective-permute-start.3
  61.7 2.2 %collective-permute-done.4.by_grp = f32[2,64,128]{2,1,0:T(8,128)S(1)} collective-permute-done((f32[2,64,128]{2,1,0:T(8,128)S(1)}, f32[2,64,128]{2,1,0:T(8,128)S(1)}, u32[]{:S(2)}, u32[]{:S(2)}) %collective-permute-start.4) | collective-permute-done | bytes 65568 | tf_op jit(solution)/shard_map/ppermute | solution.py:596
  64.0 1.7 %collective-permute-done.5.by_both = f32[2,64,128]{2,1,0:T(8,128)S(1)} collective-permute-done((f32[2,64,128]{2,1,0:T(8,128)S(1)}, f32[2,64,128]{2,1,0:T(8,128)S(1)}, u32[]{:S(2)}, u32[]{:S(2)}) %collective-permute-start.5) | collective-permute-done | bytes 65568 | tf_op jit(solution)/shard_map/ppermute | solution.py:596
  65.6 0.4 collective-permute-done.3.by_row
  66.0 0.8 %assemble.1 = f32[4,2,64,128]{3,2,1,0:T(8,128)} custom-call(f32[2,64,128]{2,1,0:T(8,128)S(1)} %pad_maximum_fusion.own, f32[2,64,128]{2,1,0:T(8,128)S(1)} %collective-permute-done.3.by_row, f32[2,64,128]{2,1,0:T(8,128)S(1)} %collective-permute-done.4.by_grp, f32[2,64,128]{2,1,0:T(8,128)S(1)} %collective-permute-done.5.by_both), custom_call_target="tpu_custom_call" | custom-call | tf_op jit(solution)/shard_map/assemble/pallas_call | solution.py:537
  (5 shorter events, 0.0 us)
Async XLA Ops:
  0.0 1.8 %collective-permute-start = (f32[512,128]{1,0:T(8,128)}, f32[512,128]{1,0:T(8,128)S(1)}, u32[]{:S(2)}, u32[]{:S(2)}) collective-permute-start(f32[512,128]{1,0:T(8,128)} %bitcast.7), channel_id=1, source_target_pairs={{0,16},{16,0},{1,17},{17,1},{2,18},{18,2},{3,19},{19,3},{4,20},{20... | collective-permute-start | bytes 786440 | tf_op jit(solution)/shard_map/ppermute | solution.py:581
  0.0 2.1 %collective-permute-start.1 = (f32[512,128]{1,0:T(8,128)}, f32[512,128]{1,0:T(8,128)S(1)}, u32[]{:S(2)}, u32[]{:S(2)}) collective-permute-start(f32[512,128]{1,0:T(8,128)} %bitcast.9), channel_id=1, source_target_pairs={{0,16},{16,0},{1,17},{17,1},{2,18},{18,2},{3,19},{19,3},{4,20},{20... | collective-permute-start | bytes 786440 | tf_op jit(solution)/shard_map/ppermute | solution.py:582
  56.7 1.3 %collective-permute-start.2 = (f32[2,64,128]{2,1,0:T(8,128)S(1)}, f32[2,64,128]{2,1,0:T(8,128)S(1)}, u32[]{:S(2)}, u32[]{:S(2)}) collective-permute-start(f32[2,64,128]{2,1,0:T(8,128)S(1)} %slice.21), channel_id=1, source_target_pairs={{0,16},{16,0},{1,17},{17,1},{2,18},{18,2},{3,19},{19,3},{4,20},{20... | collective-permute-start | bytes 196616 | tf_op jit(solution)/shard_map/ppermute | solution.py:591
  58.1 5.9 %collective-permute-start.4 = (f32[2,64,128]{2,1,0:T(8,128)S(1)}, f32[2,64,128]{2,1,0:T(8,128)S(1)}, u32[]{:S(2)}, u32[]{:S(2)}) collective-permute-start(f32[2,64,128]{2,1,0:T(8,128)S(1)} %pad_maximum_fusion.own), channel_id=1, source_target_pairs={{0,64},{32,96},{64,0},{96,32},{1,65},{33,97},{65,1},{97,33},{2,66}... | collective-permute-start | bytes 196616 | tf_op jit(solution)/shard_map/ppermute | solution.py:596
  60.2 5.5 %collective-permute-start.5 = (f32[2,64,128]{2,1,0:T(8,128)S(1)}, f32[2,64,128]{2,1,0:T(8,128)S(1)}, u32[]{:S(2)}, u32[]{:S(2)}) collective-permute-start(f32[2,64,128]{2,1,0:T(8,128)S(1)} %pad_maximum_fusion.1), channel_id=1, source_target_pairs={{0,96},{32,64},{64,32},{96,0},{1,97},{33,65},{65,33},{97,1},{2,98}... | collective-permute-start | bytes 196616 | tf_op jit(solution)/shard_map/ppermute | solution.py:596
  61.7 4.3 %collective-permute-start.3 = (f32[2,64,128]{2,1,0:T(8,128)S(1)}, f32[2,64,128]{2,1,0:T(8,128)S(1)}, u32[]{:S(2)}, u32[]{:S(2)}) collective-permute-start(f32[2,64,128]{2,1,0:T(8,128)S(1)} %pad_maximum_fusion.1), channel_id=1, source_target_pairs={{0,32},{32,0},{64,96},{96,64},{1,33},{33,1},{65,97},{97,65},{2,34}... | collective-permute-start | bytes 196616 | tf_op jit(solution)/shard_map/ppermute | solution.py:596
